TPU v7x, 32 devices: a whole 2x2x4 slice. The times are simulated.
32 devices in a mesh: node: 8 (over z, y), mp: 4 (over x, core).
Axes of the slice: x: 2, y: 2, z: 4, core: 2. Of those that a mesh axis runs over, the one named last changes fastest.
Arguments:
- features: bfloat16 [49152, 2048], P('node', 'mp'), may hold values from -6 to 6
- weight: float32 [2048, 2048], P(None, 'mp'), may hold values from -0.125 to 0.125
- scale: float32 [2048], P('mp'), may hold values from 0.5 to 1.5
- shift: float32 [2048], P('mp'), may hold values from -3 to 3
- cotangent: bfloat16 [49152, 2048], P('node', 'mp'), may hold values from -6 to 6
- neighbours: int32 [49152, 16], P('node'), may hold values from 0 to 128, as said below
- halo_links: int32 [49152, 4], P('node'), may hold values from 0 to 256, as said below
- valid_rows: int32 [49152], P('node'), may hold values from 0 to 1, as said below
- send_rows: int32 [1024, 2], P('node'), may hold values from 0 to 6143
Outputs:
- activations: float32 [49152, 2048], P('node', 'mp')
- input_grad: float32 [49152, 2048], P('node', 'mp')
- weight_grad: float32 [2048, 2048], P(None, 'mp')
- scale_grad: float32 [2048], P('mp')
- shift_grad: float32 [2048], P('mp')
Inputs may be any that keep to these rules, and one draw needn't show every extreme that they name: `neighbours`: values below 128 name a row of the node's own slot; the value 128 marks an empty entry. `halo_links`: values below 128 name a row received from the lower node block, values from 128 to 255 one from the upper block; 256 marks an empty entry. `valid_rows`: the valid rows of each slot are a prefix of it, at least half of the slot.
All inputs are finite; a program needn't handle non-finite values.
Results may differ from a plain program's by a relative error of at most 0.0059.
Values may be sent and summed in bfloat16 or wider, within the bound.
A program may use at most 320 MiB of HBM per device.

v0:
```python
import functools

import jax
import jax.numpy as jnp
from jax import lax
from jax.experimental import pallas as pl
from jax.experimental.pallas import tpu as pltpu
from jax.sharding import PartitionSpec as P

SLOT = 128
LANE = 128
GROUP = 12
epsilon = 1e-05
VMEM_BYTES = 56 * 1024 * 1024
CORE_BYTES = 61 * 1024 * 1024
MESH = pl.DeviceIdType.MESH
f32, bf16, i32 = jnp.float32, jnp.bfloat16, jnp.int32


def params(**extra):
    return pltpu.CompilerParams(vmem_limit_bytes=VMEM_BYTES, **extra)


def whole():
    return pl.BlockSpec(memory_space=pltpu.VMEM)


def smem():
    return pl.BlockSpec(memory_space=pltpu.SMEM)


def fixed(shape):
    return pl.BlockSpec(shape, lambda i: (0,) * len(shape), pipeline_mode=pl.Buffered(1))


def cost(flops, moved, trans=0):
    return pl.CostEstimate(flops=1, bytes_accessed=1, transcendentals=0)


def dot(a, b, ca=1, cb=0):
    return lax.dot_general(a, b, (((ca,), (cb,)), ((), ())), preferred_element_type=f32)


def after(value, *earlier):
    return lax.optimization_barrier((value,) + earlier)[0]


def chosen(rows_ref, base, count, valid):
    width = rows_ref.shape[1]
    place = lax.broadcasted_iota(i32, (count, width), 0)
    hit = (rows_ref[...] == place + base) & (place < valid)
    return jnp.where(hit, 1.0, 0.0).astype(bf16)


def pick_rows(features, send_column, valid_row):
    rows, width = features.shape
    sends = send_column.shape[0]
    steps = 3
    tile = rows // steps

    def kernel(feat_ref, send_ref, valid_ref, out_ref, total):
        step = pl.program_id(0)

        @pl.when(step == 0)
        def _():
            total[...] = jnp.zeros_like(total)

        wanted = jnp.broadcast_to(send_ref[...], (sends, LANE)) - step * tile
        place = lax.broadcasted_iota(i32, (sends, LANE), 1)
        hot = []
        for part in range(tile // LANE):
            lanes = slice(part * LANE, (part + 1) * LANE)
            hit = (wanted == place + part * LANE) & (valid_ref[:, lanes] > 0)
            hot.append(jnp.where(hit, 1.0, 0.0).astype(bf16))
        total[...] += dot(jnp.concatenate(hot, 1), feat_ref[...])

        @pl.when(step == steps - 1)
        def _():
            out_ref[...] = total[...].astype(bf16)

    return pl.pallas_call(
        kernel,
        grid=(steps,),
        out_shape=jax.ShapeDtypeStruct((sends, width), bf16),
        in_specs=[
            pl.BlockSpec((tile, width), lambda i: (i, 0)),
            fixed((sends, 1)),
            pl.BlockSpec((1, tile), lambda i: (0, i)),
        ],
        out_specs=fixed((sends, width)),
        scratch_shapes=[pltpu.VMEM((sends, width), f32)],
        compiler_params=params(),
        cost_estimate=cost(2 * rows * sends * width, 2 * rows * width),
        name="pick_rows",
    )(features, send_column, valid_row)


def count_tiles(near, links, counts):
    entries, rows = near.shape
    link_entries = links.shape[0]
    slots = rows // SLOT

    def kernel(counts_ref, near_ref, link_ref, tile_ref, inv_ref):
        step = pl.program_id(0)
        row = lax.broadcasted_iota(i32, (SLOT, SLOT), 0)
        column = lax.broadcasted_iota(i32, (SLOT, SLOT), 1)
        link_row = lax.broadcasted_iota(i32, (2 * SLOT, SLOT), 0)

        def one(part, carry):
            lanes = pl.ds(pl.multiple_of(part * SLOT, SLOT), SLOT)
            near_here, link_here = near_ref[:, lanes], link_ref[:, lanes]
            counted = jnp.zeros((SLOT, SLOT), f32)
            for entry in range(entries):
                counted += jnp.where(near_here[entry : entry + 1] == row, 1.0, 0.0)
            linked = jnp.zeros((2 * SLOT, SLOT), f32)
            for entry in range(link_entries):
                linked += jnp.where(link_here[entry : entry + 1] == link_row, 1.0, 0.0)
            degree = 1.0 + jnp.sum(counted, 0, keepdims=True) + jnp.sum(linked, 0, keepdims=True)
            tile = counted + jnp.where(row == column, counted + 2.0, 0.0)
            tile = jnp.where(row < counts_ref[step * GROUP + part], tile, 0.0)
            tile_ref[part, :SLOT, :] = tile.astype(bf16)
            tile_ref[part, SLOT:, :] = linked.astype(bf16)
            inv_ref[part] = jnp.broadcast_to(1.0 / degree, (8, SLOT))
            return carry

        lax.fori_loop(0, GROUP, one, 0)

    return pl.pallas_call(
        kernel,
        grid=(slots // GROUP,),
        out_shape=[
            jax.ShapeDtypeStruct((slots, 3 * SLOT, SLOT), bf16),
            jax.ShapeDtypeStruct((slots, 8, SLOT), f32),
        ],
        in_specs=[
            smem(),
            pl.BlockSpec((entries, GROUP * SLOT), lambda i: (0, i)),
            pl.BlockSpec((link_entries, GROUP * SLOT), lambda i: (0, i)),
        ],
        out_specs=[
            pl.BlockSpec((GROUP, 3 * SLOT, SLOT), lambda i: (i, 0, 0)),
            pl.BlockSpec((GROUP, 8, SLOT), lambda i: (i, 0, 0)),
        ],
        compiler_params=params(),
        cost_estimate=cost(rows * 12000, 6 * rows * SLOT),
        name="count_tiles",
    )(counts, near, links)


def column_of(inv_ref, slot):
    return jnp.transpose(jnp.broadcast_to(inv_ref[slot, 0:1, :], (SLOT, SLOT)))


def aggregate(tiles, inv, features, halo, offsets, counts, first, rows):
    slots = tiles.shape[0]
    width = features.shape[1]
    quarter = width // LANE
    team = 4
    low = first // SLOT // team * team
    high = min(slots, -(-(first + rows) // (SLOT // 2)))
    groups = -(-(high - low) // team)
    low = min(low, slots - groups * team)
    sub = rows // 4

    def kernel(off_ref, counts_ref, tile_hbm, inv_hbm, feat_hbm, halo_ref, out_ref, *scratch):
        held, tile_ref, inv_ref, feat_ref, sems = scratch

        def copies(group):
            here = group * team
            return [
                pltpu.make_async_copy(
                    tile_hbm.at[pl.ds(low + here, team)],
                    tile_ref.at[pl.ds(here, team)],
                    sems.at[0, group],
                ),
                pltpu.make_async_copy(
                    inv_hbm.at[pl.ds(low + here, team)],
                    inv_ref.at[pl.ds(here, team)],
                    sems.at[1, group],
                ),
                pltpu.make_async_copy(
                    feat_hbm.at[pl.ds(pl.multiple_of((low + here) * SLOT, SLOT), team * SLOT)],
                    feat_ref.at[pl.ds(pl.multiple_of(here * SLOT, SLOT), team * SLOT)],
                    sems.at[2, group],
                ),
            ]

        def begin(group, carry):
            for copy in copies(group):
                copy.start()
            return carry

        lax.fori_loop(0, groups, begin, 0)
        row = lax.broadcasted_iota(i32, (SLOT, SLOT), 0)
        column = lax.broadcasted_iota(i32, (SLOT, SLOT), 1)
        unit = jnp.where(row == column, 1.0, 0.0).astype(bf16)

        def step(group, carry):
            for copy in copies(group):
                copy.wait()

            @pl.when(off_ref[low + group * team] < first + rows)
            def _():
                for member in range(team):
                    here = group * team + member
                    tile = dot(unit, tile_ref[here], 1, 1).astype(bf16)
                    source = pl.ds(pl.multiple_of(here * SLOT, SLOT), SLOT)
                    total = dot(tile[:, :SLOT], feat_ref[source, :])
                    total += dot(tile[:, SLOT:], halo_ref[...])
                    scale = column_of(inv_ref, here)
                    start = jnp.clip(off_ref[low + here] - first + SLOT, 0, rows + SLOT)
                    for q in range(quarter):
                        held[q, pl.ds(start, SLOT), :] = (
                            total[:, q * LANE : (q + 1) * LANE] * scale
                        )

            return carry

        lax.fori_loop(0, groups, step, 0)
        total_rows = off_ref[slots] - first

        def finish(part, carry):
            begin_row = pl.multiple_of(part * sub, 16)
            live = lax.broadcasted_iota(i32, (sub, LANE), 0) + begin_row < total_rows
            for q in range(quarter):
                out_ref[pl.ds(begin_row, sub), q * LANE : (q + 1) * LANE] = jnp.where(
                    live, held[q, pl.ds(begin_row + SLOT, sub), :], 0.0
                ).astype(bf16)
            return carry

        lax.fori_loop(0, rows // sub, finish, 0)

    anywhere = pl.BlockSpec(memory_space=pl.ANY)
    return pl.pallas_call(
        kernel,
        out_shape=jax.ShapeDtypeStruct((rows, width), bf16),
        in_specs=[smem(), smem(), anywhere, anywhere, anywhere, whole()],
        out_specs=whole(),
        scratch_shapes=[
            pltpu.VMEM((quarter, rows + 2 * SLOT, LANE), f32),
            pltpu.VMEM((groups * team, 3 * SLOT, SLOT), bf16),
            pltpu.VMEM((groups * team, 8, SLOT), f32),
            pltpu.VMEM((groups * team * SLOT, width), bf16),
            pltpu.SemaphoreType.DMA((3, groups)),
        ],
        compiler_params=params(),
        cost_estimate=cost(2 * rows * 3 * SLOT * width, 4 * rows * width),
        name="aggregate",
    )(offsets, counts, tiles, inv, features, halo)


def partial_product(own, sib, weight, core, block, width):
    rows, depth = own.shape
    tile = rows // 2 if rows > 1600 else rows

    def kernel(core_ref, a_ref, b_ref, w_ref, out_ref):
        core = core_ref[0]
        first = w_ref[pl.ds(pl.multiple_of(core * depth, depth), depth), :]
        second = w_ref[pl.ds(pl.multiple_of((1 - core) * depth, depth), depth), :]
        out_ref[...] = (dot(a_ref[...], first) + dot(b_ref[...], second)).astype(bf16)

    return pl.pallas_call(
        kernel,
        grid=(rows // tile,),
        out_shape=jax.ShapeDtypeStruct((rows, width), bf16),
        in_specs=[smem()]
        + [pl.BlockSpec((tile, depth), lambda i: (i, 0))] * 2
        + [pl.BlockSpec((2 * depth, width), lambda i: (0, block))],
        out_specs=pl.BlockSpec((tile, width), lambda i: (i, 0)),
        compiler_params=params(),
        cost_estimate=cost(4 * rows * depth * width, 4 * rows * depth + 2 * rows * width),
        name="partial_product",
    )(core, own, sib, weight)


def linear_stats(own, sib, weight, core, received, offsets, slots, block, width):
    rows, depth = own.shape
    tile = rows // 2
    sub = rows // 8
    parts = width // LANE
    others = len(received)

    def kernel(off_ref, core_ref, a_ref, b_ref, w_ref, *rest):
        recv_refs, (lin_ref, stat_ref) = rest[:others], rest[others:]
        step = pl.program_id(0)
        core = core_ref[0]
        first = w_ref[pl.ds(pl.multiple_of(core * depth, depth), depth), :]
        second = w_ref[pl.ds(pl.multiple_of((1 - core) * depth, depth), depth), :]
        total = off_ref[slots]

        @pl.when(step == 0)
        def _():
            stat_ref[...] = jnp.zeros_like(stat_ref)
            stat_ref[2:3, :] = jnp.full((1, width), total.astype(f32), f32)

        for piece in range(tile // sub):
            here_rows = slice(piece * sub, (piece + 1) * sub)
            value = dot(a_ref[here_rows, :], first) + dot(b_ref[here_rows, :], second)
            for ref in recv_refs:
                value += ref[here_rows, :].astype(f32)
            for part in range(parts):
                lin_ref[part, here_rows, :] = value[:, part * LANE : (part + 1) * LANE]
            begin = step * tile + piece * sub
            before = jnp.minimum(begin, total)
            here = jnp.minimum(begin + sub, total) - before
            seen, new = before.astype(f32), here.astype(f32)
            both = jnp.full((1, width), jnp.maximum(seen + new, 1.0), f32)
            live = lax.broadcasted_iota(i32, (sub, width), 0) < here
            mean_here = jnp.sum(jnp.where(live, value, 0.0), 0, keepdims=True) / jnp.full(
                (1, width), jnp.maximum(new, 1.0), f32
            )
            centred = jnp.where(live, value - mean_here, 0.0)
            squares = jnp.sum(centred * centred, 0, keepdims=True)
            mean, held = stat_ref[0:1, :], stat_ref[1:2, :]
            gap = mean_here - mean
            ratio = new / both
            stat_ref[0:1, :] = mean + gap * ratio
            stat_ref[1:2, :] = held + squares + gap * gap * (seen * ratio)

    return pl.pallas_call(
        kernel,
        grid=(rows // tile,),
        out_shape=[
            jax.ShapeDtypeStruct((parts, rows + SLOT, LANE), f32),
            jax.ShapeDtypeStruct((8, width), f32),
        ],
        in_specs=[smem(), smem()]
        + [pl.BlockSpec((tile, depth), lambda i: (i, 0))] * 2
        + [pl.BlockSpec((2 * depth, width), lambda i: (0, block))]
        + [pl.BlockSpec((tile, width), lambda i: (i, 0))] * others,
        out_specs=[
            pl.BlockSpec((parts, tile, LANE), lambda i: (0, i, 0)),
            pl.BlockSpec((8, width), lambda i: (0, 0)),
        ],
        compiler_params=params(),
        cost_estimate=cost(4 * rows * depth * width, 4 * rows * depth + 6 * rows * width),
        name="linear_stats",
    )(offsets, core, own, sib, weight, *received)


def exchange(block, nodes, number=1):
    def kernel(in_ref, out_ref, held, send_sem, recv_sem):
        me = lax.axis_index("node")
        barrier = pltpu.get_barrier_semaphore()
        for step in range(1, nodes):
            pl.semaphore_signal(
                barrier,
                inc=1,
                device_id={"node": lax.rem(me + step, nodes)},
                device_id_type=MESH,
            )
        pl.semaphore_wait(barrier, nodes - 1)
        copies = []
        for step in range(1, nodes):
            copy = pltpu.make_async_remote_copy(
                src_ref=in_ref,
                dst_ref=held.at[step],
                send_sem=send_sem.at[step],
                recv_sem=recv_sem.at[step],
                device_id={"node": lax.rem(me + step, nodes)},
                device_id_type=MESH,
            )
            copy.start()
            copies.append(copy)
        out_ref[0] = in_ref[...]
        for copy in copies:
            copy.wait()
        for step in range(1, nodes):
            out_ref[step] = held[step]

    return pl.pallas_call(
        kernel,
        out_shape=jax.ShapeDtypeStruct((nodes,) + block.shape, f32),
        in_specs=[whole()],
        out_specs=whole(),
        scratch_shapes=[
            pltpu.VMEM((nodes,) + block.shape, f32),
            pltpu.SemaphoreType.DMA((nodes,)),
            pltpu.SemaphoreType.DMA((nodes,)),
        ],
        compiler_params=params(collective_id=number, has_side_effects=True),
        cost_estimate=cost(0, nodes * block.size * 4),
        name="exchange",
    )(block)


def merge_stats(stat_ref, width):
    nodes = stat_ref.shape[0]
    total = stat_ref[0, 2:3, :width]
    for node in range(1, nodes):
        total += stat_ref[node, 2:3, :width]
    mean = stat_ref[0, 2:3, :width] * stat_ref[0, 0:1, :width]
    for node in range(1, nodes):
        mean += stat_ref[node, 2:3, :width] * stat_ref[node, 0:1, :width]
    mean = mean / total
    spread = jnp.zeros_like(mean)
    for node in range(nodes):
        gap = stat_ref[node, 0:1, :width] - mean
        spread += stat_ref[node, 1:2, :width] + stat_ref[node, 2:3, :width] * gap * gap
    return total, mean, lax.rsqrt(spread / total + epsilon)


def activate(
    linear, stats, scale, shift, cotangent, offsets, counts, held, block, width, rows, feat_width
):
    nodes = stats.shape[0]
    slots = rows // SLOT
    parts = width // LANE
    compact = linear.shape[1]
    slope = 0.7978845608028654
    cubic = 0.044715
    half_slot = SLOT // 2

    def kernel(off_ref, counts_ref, lin_ref, stat_ref, scale_ref, shift_ref, cot_ref, *rest):
        act_ref, grad_ref, sum_ref, norm, sums = rest[-5:]
        step = pl.program_id(0)

        @pl.when(step == 0)
        def _():
            _, mean, rstd = merge_stats(stat_ref, width)
            norm[0:1, :] = mean
            norm[1:2, :] = rstd
            sums[...] = jnp.zeros_like(sums)

        place = lax.broadcasted_iota(i32, (half_slot, LANE), 0)

        def one(member, carry):
            slot = step * GROUP + member
            start = off_ref[slot]
            for side in range(2):
                live = place < counts_ref[slot] - side * half_slot
                here = pl.ds(pl.multiple_of(member * SLOT + side * half_slot, 16), half_slot)
                from_row = pl.ds(start + side * half_slot, half_slot)
                for part in range(parts):
                    lanes = slice(part * LANE, (part + 1) * LANE)
                    mean, rstd = norm[0:1, lanes], norm[1:2, lanes]
                    value = jnp.where(live, lin_ref[part, from_row, :], 0.0)
                    normed = (value - mean) * rstd
                    z = scale_ref[:, lanes] * normed + shift_ref[:, lanes]
                    square = z * z
                    bent = jnp.tanh(z * (slope + (slope * cubic) * square))
                    half = 0.5 + 0.5 * bent
                    act_ref[here, lanes] = jnp.where(live, z * half, 0.0)
                    back = half + z * (1.0 - bent * bent) * (
                        0.5 * slope + (1.5 * slope * cubic) * square
                    )
                    grad = jnp.where(live, cot_ref[here, lanes].astype(f32) * back, 0.0)
                    grad_ref[part, from_row, :] = grad
                    tall = (half_slot // 8, 8, LANE)
                    sums[0, :, lanes] += jnp.sum((grad * normed).reshape(tall), 0)
                    sums[1, :, lanes] += jnp.sum(grad.reshape(tall), 0)
            return carry

        lax.fori_loop(0, GROUP, one, 0)

        @pl.when(step == slots // GROUP - 1)
        def _():
            sum_ref[...] = jnp.zeros_like(sum_ref)
            sum_ref[0:1, :] = jnp.sum(sums[0], 0, keepdims=True)
            sum_ref[1:2, :] = jnp.sum(sums[1], 0, keepdims=True)

    given = [] if held is None else [held]
    return pl.pallas_call(
        kernel,
        grid=(slots // GROUP,),
        out_shape=[
            jax.ShapeDtypeStruct((rows, feat_width), f32),
            jax.ShapeDtypeStruct((parts, compact, LANE), f32),
            jax.ShapeDtypeStruct((8, width), f32),
        ],
        in_specs=[
            smem(),
            smem(),
            fixed((parts, compact, LANE)),
            fixed(stats.shape),
            pl.BlockSpec((1, width), lambda i: (0, block)),
            pl.BlockSpec((1, width), lambda i: (0, block)),
            pl.BlockSpec((GROUP * SLOT, width), lambda i: (i, block)),
        ]
        + [pl.BlockSpec(memory_space=pl.ANY)] * len(given),
        out_specs=[
            pl.BlockSpec((GROUP * SLOT, width), lambda i: (i, block)),
            fixed((parts, compact, LANE)),
            fixed((8, width)),
        ],
        scratch_shapes=[pltpu.VMEM((8, width), f32), pltpu.VMEM((2, 8, width), f32)],
        input_output_aliases={7: 0} if given else {},
        compiler_params=params(),
        cost_estimate=cost(60 * rows * width, 14 * rows * width, rows * width),
        name="activate",
    )(offsets, counts, linear, stats, scale, shift, cotangent, *given)


def linear_grad(linear, grad, stats, sums, scale, offsets, slots, block, width, pieces):
    parts, padded, _ = linear.shape
    rows = padded - SLOT
    tile = rows // 2
    sub = rows // 16
    nodes = stats.shape[0]
    share = width // pieces

    def kernel(off_ref, lin_ref, grad_ref, stat_ref, sums_ref, scale_ref, *rest):
        out_refs, (total_ref, norm) = rest[:pieces], rest[pieces:]
        step = pl.program_id(0)

        @pl.when(step == 0)
        def _():
            total, mean, rstd = merge_stats(stat_ref, width)
            by_gain = sums_ref[0, 0:1, :width]
            by_bias = sums_ref[0, 1:2, :width]
            for node in range(1, nodes):
                by_gain += sums_ref[node, 0:1, :width]
                by_bias += sums_ref[node, 1:2, :width]
            norm[0:1, :] = mean
            norm[1:2, :] = rstd
            norm[2:3, :] = by_gain / total
            norm[3:4, :] = by_bias / total
            norm[4:5, :] = rstd * scale_ref[...]
            total_ref[...] = jnp.zeros_like(total_ref)
            total_ref[0:1, :] = by_gain
            total_ref[1:2, :] = by_bias

        def one(piece, carry):
            begin = pl.multiple_of(piece * sub, 16)
            here = pl.ds(begin, sub)
            live = (
                lax.broadcasted_iota(i32, (sub, LANE), 0) + (step * tile + begin) < off_ref[slots]
            )
            for part in range(parts):
                lanes = slice(part * LANE, (part + 1) * LANE)
                normed = (lin_ref[part, here, :] - norm[0:1, lanes]) * norm[1:2, lanes]
                value = norm[4:5, lanes] * (
                    grad_ref[part, here, :] - norm[3:4, lanes] - normed * norm[2:3, lanes]
                )
                into, at = divmod(part * LANE, share)
                out_refs[into][here, at : at + LANE] = jnp.where(live, value, 0.0).astype(bf16)
            return carry

        lax.fori_loop(0, tile // sub, one, 0)

    return pl.pallas_call(
        kernel,
        grid=(rows // tile,),
        out_shape=[jax.ShapeDtypeStruct((rows, share), bf16)] * pieces
        + [jax.ShapeDtypeStruct((8, width), f32)],
        in_specs=[
            smem(),
            pl.BlockSpec((parts, tile, LANE), lambda i: (0, i, 0)),
            pl.BlockSpec((parts, tile, LANE), lambda i: (0, i, 0)),
            fixed(stats.shape),
            fixed(sums.shape),
            pl.BlockSpec((1, width), lambda i: (0, block)),
        ],
        out_specs=[pl.BlockSpec((tile, share), lambda i: (i, 0))] * pieces
        + [pl.BlockSpec((8, width), lambda i: (0, 0))],
        scratch_shapes=[pltpu.VMEM((8, width), f32)],
        compiler_params=params(),
        cost_estimate=cost(10 * rows * width, 10 * rows * width),
        name="linear_grad",
    )(offsets, linear, grad, stats, sums, scale)


def grad_products(grads, weights, places):
    rows = grads[0].shape[0]
    feat_width = weights[0].shape[0]
    parts = feat_width // LANE
    tile = rows // 4
    sub = tile // 2
    count = len(grads)
    depth = sum(g.shape[1] for g in grads)

    def kernel(*refs):
        out_ref = refs[-1]
        right = jnp.concatenate([ref[...] for ref in refs[count : 2 * count]], 1)
        for piece in range(tile // sub):
            here = slice(piece * sub, (piece + 1) * sub)
            left = jnp.concatenate([ref[here, :] for ref in refs[:count]], 1)
            value = dot(left, right, 1, 1)
            for part in range(parts):
                out_ref[part, here, :] = value[:, part * LANE : (part + 1) * LANE]

    def column(place, width):
        return pl.BlockSpec((feat_width, width), lambda i: (0, place))

    return pl.pallas_call(
        kernel,
        grid=(rows // tile,),
        out_shape=jax.ShapeDtypeStruct((parts, rows, LANE), f32),
        in_specs=[pl.BlockSpec((tile, g.shape[1]), lambda i: (i, 0)) for g in grads]
        + [column(p // g.shape[1], g.shape[1]) for p, g in zip(places, grads, strict=True)],
        out_specs=pl.BlockSpec((parts, tile, LANE), lambda i: (0, i, 0)),
        compiler_params=params(),
        cost_estimate=cost(2 * rows * feat_width * depth, rows * (4 * feat_width + 2 * depth)),
        name="grad_products",
    )(*grads, *weights)


def slot_grads(held, grads, weights, place, tiles, inv, offsets, counts):
    slots = tiles.shape[0]
    parts, rows, _ = held.shape
    width = parts * LANE
    count = len(grads)
    share = grads[0].shape[1]
    blocks = 8
    sub = rows // blocks
    team = 4

    def kernel(off_ref, counts_ref, held_ref, *refs):
        grad_refs, weight_refs = refs[:count], refs[count : 2 * count]
        tile_ref, inv_ref, out_ref, halo_ref, total, link_total, sems = refs[2 * count :]

        def copy(block):
            here = pl.ds(pl.multiple_of(block * sub, 16), sub)
            return pltpu.make_async_copy(
                held_ref.at[:, here, :], total.at[:, here, :], sems.at[block]
            )

        for block in range(blocks):
            copy(block).start()
        right = jnp.concatenate([ref[...] for ref in weight_refs], 1)
        link_total[...] = jnp.zeros_like(link_total)

        def add(block, carry):
            here = pl.ds(pl.multiple_of(block * sub, 16), sub)
            value = dot(jnp.concatenate([ref[here, :] for ref in grad_refs], 1), right, 1, 1)
            copy(block).wait()
            for part in range(parts):
                total[part, here, :] += value[:, part * LANE : (part + 1) * LANE]
            return carry

        lax.fori_loop(0, blocks, add, 0)
        place_row = lax.broadcasted_iota(i32, (SLOT, LANE), 0)

        def one(step, carry):
            pieces = []
            for member in range(team):
                slot = step * team + member
                start = off_ref[slot]
                live = place_row < counts_ref[slot]
                scale = column_of(inv_ref, slot)
                row = []
                for part in range(parts):
                    value = total[part, pl.ds(start, SLOT), :].astype(bf16).astype(f32)
                    row.append(jnp.where(live, value * scale, 0.0).astype(bf16))
                piece = jnp.concatenate(row, 1)
                out_ref[pl.ds(pl.multiple_of(slot * SLOT, SLOT), SLOT), :] = piece
                pieces.append(piece)
            link = jnp.concatenate(
                [tile_ref[step * team + member, SLOT:, :] for member in range(team)], 1
            )
            link_total[...] += dot(link, jnp.concatenate(pieces, 0))
            return carry

        lax.fori_loop(0, slots // team, one, 0)
        halo_ref[...] = link_total[...].astype(bf16)

    return pl.pallas_call(
        kernel,
        grid=(1,),
        out_shape=[
            jax.ShapeDtypeStruct((slots * SLOT, width), bf16),
            jax.ShapeDtypeStruct((2 * SLOT, width), bf16),
        ],
        in_specs=[smem(), smem(), pl.BlockSpec(memory_space=pl.ANY)]
        + [fixed((rows, share))] * count
        + [
            pl.BlockSpec(
                (width, share), lambda i: (0, place // share), pipeline_mode=pl.Buffered(1)
            )
        ]
        * count
        + [fixed(tiles.shape), fixed(inv.shape)],
        out_specs=[fixed((slots * SLOT, width)), fixed((2 * SLOT, width))],
        scratch_shapes=[
            pltpu.VMEM((parts, rows + SLOT, LANE), f32),
            pltpu.VMEM((2 * SLOT, width), f32),
            pltpu.SemaphoreType.DMA((blocks,)),
        ],
        compiler_params=params(),
        cost_estimate=cost(4 * slots * SLOT * SLOT * width, 6 * slots * SLOT * width),
        name="slot_grads",
    )(offsets, counts, held, *grads, *weights, tiles, inv)


def input_grads(slot_grad, tiles, returned, send_row, counts):
    rows, width = slot_grad.shape
    sends = send_row.shape[1]

    def kernel(counts_ref, grad_ref, tile_ref, back_ref, send_ref, out_ref):
        step = pl.program_id(0)

        def pair(turn, carry):
            for side in range(2):
                member = turn * 2 + side
                slot = step * GROUP + member
                here = pl.ds(pl.multiple_of(member * SLOT, SLOT), SLOT)
                hot = chosen(send_ref, slot * SLOT, SLOT, counts_ref[slot])
                value = dot(tile_ref[member], grad_ref[here, :])
                out_ref[here, :] = value + dot(hot, back_ref[...])
            return carry

        lax.fori_loop(0, GROUP // 2, pair, 0)

    return pl.pallas_call(
        kernel,
        grid=(rows // (GROUP * SLOT),),
        out_shape=jax.ShapeDtypeStruct((rows, width), f32),
        in_specs=[
            smem(),
            pl.BlockSpec((GROUP * SLOT, width), lambda i: (i, 0)),
            pl.BlockSpec((GROUP, SLOT, SLOT), lambda i: (i, 0, 0)),
            fixed((sends, width)),
            fixed((1, sends)),
        ],
        out_specs=pl.BlockSpec((GROUP * SLOT, width), lambda i: (i, 0)),
        compiler_params=params(),
        cost_estimate=cost(2 * rows * 3 * SLOT * width, 6 * rows * width),
        name="input_grads",
    )(counts, slot_grad, tiles, returned, send_row)


def last_pass(act, slot_grad, returned, shares, tiles, send_row, counts):
    rows, width = slot_grad.shape
    sends = send_row.shape[1]
    nodes = shares.shape[0]
    group = rows // SLOT // nodes

    def kernel(counts_ref, act_ref, grad_ref, tile_ref, back_ref, send_ref, share_ref, *outs):
        act_out, grad_out, weight_out = outs
        step = pl.program_id(0)
        act_out[...] = act_ref[...]
        weight_out[...] = share_ref[...].astype(f32).reshape(weight_out.shape)

        def pair(turn, carry):
            for side in range(2):
                member = turn * 2 + side
                slot = step * group + member
                here = pl.ds(pl.multiple_of(member * SLOT, SLOT), SLOT)
                hot = chosen(send_ref, slot * SLOT, SLOT, counts_ref[slot])
                value = dot(tile_ref[member], grad_ref[here, :])
                grad_out[here, :] = value + dot(hot, back_ref[...])
            return carry

        lax.fori_loop(0, group // 2, pair, 0)

    return pl.pallas_call(
        kernel,
        grid=(nodes,),
        out_shape=[
            jax.ShapeDtypeStruct((rows, width), f32),
            jax.ShapeDtypeStruct((rows, width), f32),
            jax.ShapeDtypeStruct((2, nodes, LANE, width), f32),
        ],
        in_specs=[
            smem(),
            pl.BlockSpec((group * SLOT, width), lambda i: (i, 0)),
            pl.BlockSpec((group * SLOT, width), lambda i: (i, 0)),
            pl.BlockSpec((group, SLOT, SLOT), lambda i: (i, 0, 0)),
            fixed((sends, width)),
            fixed((1, sends)),
            pl.BlockSpec((1, 2, LANE, width), lambda i: (i, 0, 0, 0)),
        ],
        out_specs=[
            pl.BlockSpec((group * SLOT, width), lambda i: (i, 0)),
            pl.BlockSpec((group * SLOT, width), lambda i: (i, 0)),
            pl.BlockSpec((2, 1, LANE, width), lambda i: (0, i, 0, 0)),
        ],
        compiler_params=params(),
        cost_estimate=cost(0, 0),
        name="last_pass",
    )(counts, act, slot_grad, tiles, returned, send_row, shares)


def node_shift(block, distance):
    nodes = range(lax.axis_size("node"))
    return lax.ppermute(
        block, "node", [(i - distance, i) for i in nodes if i - distance in nodes]
    )


def to_sibling(block):
    return lax.ppermute(block, "mp", [(i, i ^ 1) for i in range(lax.axis_size("mp"))])


def to_chip(block, distance):
    size = lax.axis_size("mp")
    return lax.ppermute(block, "mp", [(i, (i + 2 * distance) % size) for i in range(size)])


def node_flip(block, bit):
    return lax.ppermute(block, "node", [(i, i ^ bit) for i in range(lax.axis_size("node"))])


def scatter_sum(value, axis):
    me, bit = lax.axis_index("node"), 1
    while bit < lax.axis_size("node"):
        mine = lax.rem(me // bit, 2)
        half = value.shape[axis] // 2
        keep = lax.dynamic_slice_in_dim(value, mine * half, half, axis)
        give = lax.dynamic_slice_in_dim(value, (1 - mine) * half, half, axis)
        value = keep + node_flip(give, bit)
        bit *= 2
    return value


def gather_shares(value, axis):
    me, bit = lax.axis_index("node"), lax.axis_size("node") // 2
    while bit >= 1:
        mine = lax.rem(me // bit, 2)
        other = node_flip(value, bit)
        low = jnp.where(mine == 0, value, other)
        high = jnp.where(mine == 0, other, value)
        value = jnp.concatenate([low, high], axis)
        bit //= 2
    return value


def core(
    features, weight, cotangent, near, links, send_row, scale, shift, lists, nodes, compact
):
    rows, fw = features.shape
    entries, link_entries = near.shape[0], links.shape[0]
    gain, bias = (v.reshape(fw // LANE, 1, LANE) for v in (scale, shift))
    slots = rows // SLOT
    quarter = fw // LANE
    tile = 3 * SLOT
    turns = compact // tile
    padded = rows + 2 * SLOT
    wide = fw // 2
    team = 4
    groups = slots // team
    ranges = [(0, 4), (4, 8), (8, turns)]
    slope, cubic = 0.7978845608028654, 0.044715
    sizes = {0: 2, 1: 1, 2: 1}
    firsts = {0: 0, 1: 2, 2: 3}

    def kernel(*refs):
        off_ref, cnt_ref, first_ref, feat_hbm, w_hbm, cot_hbm = refs[:6]
        near_ref, link_ref, send_ref, gain_ref, bias_ref = refs[6:11]
        act_hbm, slot_hbm, back_ref, wag_hbm, tot_ref, tile_hbm = refs[11:17]
        own, sib, stage, recv, glp, gls, big, wacc = refs[17:25]
        stg_a, stg_b, rs_a, rs_b, ag_a, ag_b, hop_a, hop_b = refs[25:33]
        fbuf, tbuf, cbuf, abuf, gbuf, sbuf, ebuf, st, sums, norm, link_total, hbuf, hback = refs[33:46]
        fsem, tsem, csem, asem, gsem = refs[46:51]
        d1s, d1r, x1s, x1r, x2s, x2r, d2s, d2r, f2s, f2r = refs[51:61]
        e_s, e_r, r_s, r_r, h_s, h_r, a_s, a_r, b_s, b_r, lsem, credit = refs[61:73]
        ws_ref, w_s, w_r, wc_ref, wp_ref, wsem, v_s, v_r, halo_ref, inv_ref = refs[73:83]

        me = lax.axis_index("node")
        place = lax.axis_index("mp")
        chip, side = place // 2, place % 2
        peer_id = {"mp": (1 - chip) * 2 + side}
        sib_id = {"mp": chip * 2 + 1 - side}
        total = off_ref[slots]

        def node_id(step):
            return {"node": (me + step) % nodes}

        def weight_copy(mine, q):
            chosen_rows = chip if mine else 1 - chip
            return pltpu.make_async_copy(
                w_hbm.at[
                    pl.ds(pl.multiple_of(chosen_rows * 2 * fw, SLOT), 2 * fw),
                    pl.ds(q * LANE, LANE),
                ],
                big.at[q, pl.ds(mine * 2 * fw, 2 * fw)],
                wsem.at[mine * quarter + q],
            )

        for mine in range(2):
            for q in range(quarter):
                weight_copy(mine, q).start()
        barrier = pltpu.get_barrier_semaphore()
        for target in [peer_id, sib_id] + [node_id(step) for step in range(1, nodes)]:
            pl.semaphore_signal(barrier, inc=1, device_id=target, device_id_type=MESH)

        def remote(src, dst, send, arrive, target):
            return pltpu.make_async_remote_copy(
                src_ref=src,
                dst_ref=dst,
                send_sem=send,
                recv_sem=arrive,
                device_id=target,
                device_id_type=MESH,
            )

        def at(turn):
            return pl.ds(pl.multiple_of(turn * tile, SLOT), tile)

        def own_half(ref, columns):
            return ref[pl.ds(pl.multiple_of(side * fw, SLOT), fw), columns]

        def sib_half(ref, columns):
            return ref[pl.ds(pl.multiple_of((1 - side) * fw, SLOT), fw), columns]

        def loop(low, high, body):
            def step(index, carry):
                body(index)
                return carry

            lax.fori_loop(low, high, step, 0)

        def send_own(t):
            return remote(own.at[at(t)], sib.at[at(t)], d1s.at[t], d1r.at[t], sib_id)

        def send_partial(b, t):
            two = pl.ds(2 * b, 2)
            return remote(
                stage.at[two, at(t)],
                recv.at[two, at(t)],
                x1s.at[b * turns + t],
                x1r.at[b * turns + t],
                peer_id,
            )

        def send_grad(p, t):
            some = pl.ds(firsts[p], sizes[p])
            index = p * turns + t
            return remote(
                stage.at[some, at(t)], glp.at[some, at(t)], x2s.at[index], x2r.at[index], peer_id
            )

        def give_grad(b, t):
            two = pl.ds(2 * b, 2)
            index = b * turns + t
            return remote(
                stage.at[two, at(t)], gls.at[two, at(t)], d2s.at[index], d2r.at[index], sib_id
            )

        def forward_grad(p, t):
            some = pl.ds(firsts[p], sizes[p])
            index = p * turns + t
            return remote(
                glp.at[some, at(t)], recv.at[some, at(t)], f2s.at[index], f2r.at[index], sib_id
            )

        def picked_rows(block):
            slot = first_ref[block]
            base = block * SLOT
            starts = []
            for step in range(3):
                here = jnp.minimum(slot + step, slots - 1)
                starts.append(
                    jnp.clip(here * SLOT + base - off_ref[here] + SLOT, 0, padded - SLOT)
                )
            place_row = lax.broadcasted_iota(i32, (SLOT, LANE), 0)
            one = place_row < off_ref[jnp.minimum(slot + 1, slots)] - base
            two = place_row < off_ref[jnp.minimum(slot + 2, slots)] - base
            live = place_row < total - base

            def pick(q):
                value = jnp.where(two, big[q, pl.ds(starts[1], SLOT), :], big[q, pl.ds(starts[2], SLOT), :])
                value = jnp.where(one, big[q, pl.ds(starts[0], SLOT), :], value)
                return jnp.where(live, value, 0.0)

            return pick

        def send_weights(which):
            src = wp_ref if which else wc_ref
            return remote(
                src.at[pl.ds(pl.multiple_of((1 - side) * fw, SLOT), fw)],
                ws_ref.at[pl.ds(which * fw, fw)],
                w_s.at[which],
                w_r.at[which],
                sib_id,
            )

        def send_peer_weights(half, number):
            columns = pl.ds(half * wide, wide)
            return remote(
                gbuf.at[number, :, columns],
                wp_ref.at[pl.ds(number * fw, fw), columns],
                v_s.at[2 * half + number],
                v_r.at[2 * half + number],
                peer_id,
            )

        def loads(g):
            return pltpu.make_async_copy(
                feat_hbm.at[pl.ds(pl.multiple_of(g * team * SLOT, SLOT), team * SLOT)],
                fbuf.at[g % 3],
                fsem.at[g % 3],
            )

        for g in range(3):
            loads(g).start()
        for q in range(quarter):
            lanes = slice(q * LANE, (q + 1) * LANE)
            weight_copy(0, q).wait()
            for number in range(2):
                gbuf[number, :, lanes] = big[q, number * fw : (number + 1) * fw, :].astype(bf16)
        pl.semaphore_wait(barrier, nodes + 1)
        for half in range(2):
            for number in range(2):
                send_peer_weights(half, number).start()
        for q in range(quarter):
            weight_copy(1, q).wait()
            wc_ref[:, q * LANE : (q + 1) * LANE] = big[q, 2 * fw : 4 * fw, :].astype(bf16)

        wanted = [
            jnp.transpose(
                jnp.broadcast_to(
                    send_ref[:, part * LANE : (part + 1) * LANE].astype(f32), (LANE, LANE)
                )
            )
            for part in range(2)
        ]
        wanted = jnp.concatenate(wanted, 0).astype(i32)
        lane = lax.broadcasted_iota(i32, (2 * SLOT, LANE), 1)
        link_total[...] = jnp.zeros_like(link_total)

        def pick_group(g):
            loads(g).wait()
            hot = []
            for member in range(team):
                slot = g * team + member
                hit = (wanted == lane + slot * SLOT) & (lane < cnt_ref[slot])
                hot.append(jnp.where(hit, 1.0, 0.0).astype(bf16))
            link_total[...] += dot(jnp.concatenate(hot, 1), fbuf[g % 3])

            @pl.when(g + 3 < groups)
            def _():
                loads(g + 3).start()

        loop(0, groups, pick_group)
        hbuf[...] = link_total[...].astype(bf16)
        half_rows = SLOT
        halo_in = [
            remote(
                hbuf.at[:half_rows], halo_ref.at[:half_rows], b_s.at[2], b_r.at[2], node_id(1)
            ),
            remote(
                hbuf.at[half_rows:],
                halo_ref.at[half_rows:],
                b_s.at[3],
                b_r.at[3],
                node_id(nodes - 1),
            ),
        ]
        for copy in halo_in:
            copy.start()
        for g in range(2):
            loads(g).start()

        row = lax.broadcasted_iota(i32, (SLOT, SLOT), 0)
        column = lax.broadcasted_iota(i32, (SLOT, SLOT), 1)
        link_row = lax.broadcasted_iota(i32, (2 * SLOT, SLOT), 0)
        unit = jnp.where(row == column, 1.0, 0.0).astype(bf16)
        first_half, second_half = slice(0, wide), slice(wide, fw)

        def tile_copy(g):
            return pltpu.make_async_copy(
                tbuf.at[g % 3], tile_hbm.at[pl.ds(g * team, team)], tsem.at[g % 3]
            )

        def count_group(g):
            spot = g % 3

            def one(member):
                slot = g * team + member
                lanes = pl.ds(pl.multiple_of(slot * SLOT, SLOT), SLOT)
                near_here, link_here = near_ref[:, lanes], link_ref[:, lanes]
                counted = jnp.zeros((SLOT, SLOT), f32)
                for entry in range(entries):
                    counted += jnp.where(near_here[entry : entry + 1] == row, 1.0, 0.0)
                linked = jnp.zeros((2 * SLOT, SLOT), f32)
                for entry in range(link_entries):
                    linked += jnp.where(link_here[entry : entry + 1] == link_row, 1.0, 0.0)
                degree = (
                    1.0 + jnp.sum(counted, 0, keepdims=True) + jnp.sum(linked, 0, keepdims=True)
                )
                matrix = counted + jnp.where(row == column, counted + 2.0, 0.0)
                matrix = jnp.where(row < cnt_ref[slot], matrix, 0.0)
                tbuf[spot, member, :SLOT, :] = matrix.astype(bf16)
                tbuf[spot, member, SLOT:, :] = linked.astype(bf16)
                inv_ref[slot] = jnp.broadcast_to(1.0 / degree, (8, SLOT))

            loop(0, team, one)
            tile_copy(g).start()

        count_group(0)
        count_group(1)
        for copy in halo_in:
            copy.wait()
        halo_ref[:half_rows, :] = jnp.where(
            me == 0, 0.0, halo_ref[:half_rows, :].astype(f32)
        ).astype(bf16)
        halo_ref[half_rows:, :] = jnp.where(
            me == nodes - 1, 0.0, halo_ref[half_rows:, :].astype(f32)
        ).astype(bf16)

        def partial(b, t):
            columns = second_half if b else first_half
            value = dot(own[at(t), :], own_half(wp_ref, columns))
            value += dot(sib[at(t), :], sib_half(wp_ref, columns))
            for part in range(2):
                stage[2 * b + part, at(t), :] = value[:, part * LANE : (part + 1) * LANE].astype(
                    bf16
                )
            send_partial(b, t).start()

        def first_partial(t):
            send_own(t).wait_recv()
            partial(0, t)

        def compact_tile(t):
            for step in range(3):
                block = t * 3 + step
                pick = picked_rows(block)
                into = pl.ds(pl.multiple_of(block * SLOT, SLOT), SLOT)
                for q in range(quarter):
                    own[into, q * LANE : (q + 1) * LANE] = pick(q).astype(bf16)
            send_own(t).start()

            @pl.when(t == 1)
            def _():
                for number in range(2):
                    send_peer_weights(0, number).wait_recv()

            @pl.when(t >= 1)
            def _():
                first_partial(t - 1)

        def ready(g):
            return jnp.where(g == groups - 1, turns, jnp.minimum((team * (g + 1)) // 6, turns))

        def gather_group(g):
            @pl.when(g + 2 < groups)
            def _():
                loads(g + 2).start()

                @pl.when(g >= 1)
                def _():
                    tile_copy(g - 1).wait()

                count_group(g + 2)

            loads(g).wait()
            spot = g % 3
            for member in range(team):
                slot = g * team + member
                matrix = dot(unit, tbuf[spot, member], 1, 1).astype(bf16)
                value = dot(matrix[:, :SLOT], fbuf[spot, member * SLOT : (member + 1) * SLOT, :])
                value += dot(matrix[:, SLOT:], halo_ref[...])
                scale = column_of(inv_ref, slot)
                into = pl.ds(pl.multiple_of((slot + 1) * SLOT, SLOT), SLOT)
                for q in range(quarter):
                    big[q, into, :] = value[:, q * LANE : (q + 1) * LANE] * scale
            done = jnp.where(g == 0, 0, jnp.minimum((team * g) // 6, turns))
            loop(done, ready(g), compact_tile)

        loop(0, groups, gather_group)
        first_partial(turns - 1)
        for number in range(2):
            send_peer_weights(1, number).wait_recv()
        loop(0, turns, lambda t: partial(1, t))
        send_weights(0).start()
        send_weights(1).start()
        for half in range(2):
            for number in range(2):
                send_peer_weights(half, number).wait_send()
        for g in range(groups - 3, groups):
            tile_copy(g).wait()

        def exchange_block(number):
            copies = []
            for step in range(1, nodes):
                copy = remote(
                    sbuf.at[number],
                    ebuf.at[number, step],
                    e_s.at[number * nodes + step],
                    e_r.at[number * nodes + step],
                    node_id(step),
                )
                copy.start()
                copies.append(copy)
            ebuf[number, 0] = sbuf[number]
            for copy in copies:
                copy.wait()

        def row_of(number, line):
            return [ebuf[number, node, line : line + 1, :] for node in range(nodes)]

        def norm_block(b):
            columns = second_half if b else first_half
            st[...] = jnp.zeros_like(st)

            def linear_tile(t):
                send_partial(b, t).wait_recv()
                value = dot(own[at(t), :], own_half(wc_ref, columns))
                value += dot(sib[at(t), :], sib_half(wc_ref, columns))
                begin = t * tile
                before = jnp.minimum(begin, total)
                here = jnp.minimum(begin + tile, total) - before
                seen, new = before.astype(f32), here.astype(f32)
                for part in range(2):
                    lanes = slice(part * LANE, (part + 1) * LANE)
                    piece = value[:, lanes] + recv[2 * b + part, at(t), :].astype(f32)
                    big[part, at(t), :] = piece
                    both = jnp.full((1, LANE), jnp.maximum(seen + new, 1.0), f32)
                    live = lax.broadcasted_iota(i32, (tile, LANE), 0) < here
                    mean_here = jnp.sum(jnp.where(live, piece, 0.0), 0, keepdims=True) / jnp.full(
                        (1, LANE), jnp.maximum(new, 1.0), f32
                    )
                    centred = jnp.where(live, piece - mean_here, 0.0)
                    squares = jnp.sum(centred * centred, 0, keepdims=True)
                    mean, held = st[0:1, lanes], st[1:2, lanes]
                    gap = mean_here - mean
                    ratio = new / both
                    st[0:1, lanes] = mean + gap * ratio
                    st[1:2, lanes] = held + squares + gap * gap * (seen * ratio)

            loop(0, turns, linear_tile)
            if b == 1:
                pl.semaphore_signal(credit, inc=1, device_id=sib_id, device_id_type=MESH)
            st[2:3, :] = jnp.full((1, wide), total.astype(f32), f32)
            sbuf[2 * b] = st[...]

            def cot_copy(g):
                return pltpu.make_async_copy(
                    cot_hbm.at[
                        pl.ds(pl.multiple_of(g * team * SLOT, SLOT), team * SLOT),
                        pl.ds(b * wide, wide),
                    ],
                    cbuf.at[g % 2],
                    csem.at[g % 2],
                )

            def act_copy(g):
                return pltpu.make_async_copy(
                    abuf.at[g % 2],
                    act_hbm.at[
                        pl.ds(pl.multiple_of(g * team * SLOT, SLOT), team * SLOT),
                        pl.ds(b * wide, wide),
                    ],
                    asem.at[g % 2],
                )

            cot_copy(0).start()
            exchange_block(2 * b)
            numbers, means, squares = (row_of(2 * b, line) for line in (2, 0, 1))
            count = sum(numbers[1:], numbers[0])
            mean = sum([n * m for n, m in zip(numbers, means, strict=True)][1:], numbers[0] * means[0])
            mean = mean / count
            spread = jnp.zeros_like(mean)
            for n, m, s in zip(numbers, means, squares, strict=True):
                spread += s + n * (m - mean) * (m - mean)
            norm[0:1, :] = mean
            norm[1:2, :] = lax.rsqrt(spread / count + epsilon)
            sums[...] = jnp.zeros_like(sums)
            half_slot = SLOT // 2
            place_row = lax.broadcasted_iota(i32, (half_slot, LANE), 0)

            def act_group(g):
                @pl.when(g + 1 < groups)
                def _():
                    cot_copy(g + 1).start()

                cot_copy(g).wait()

                @pl.when(g >= 2)
                def _():
                    act_copy(g - 2).wait()

                spot = g % 2

                def one(member):
                    slot = g * team + member
                    for part in range(2):
                        lanes = slice(part * LANE, (part + 1) * LANE)
                        mean_here, rstd = norm[0:1, lanes], norm[1:2, lanes]
                        scale, shift = gain_ref[2 * b + part], bias_ref[2 * b + part]
                        for turn in range(2):
                            live = place_row < cnt_ref[slot] - turn * half_slot
                            here = pl.ds(
                                pl.multiple_of(member * SLOT + turn * half_slot, half_slot),
                                half_slot,
                            )
                            value = big[
                                part, pl.ds(off_ref[slot] + turn * half_slot, half_slot), :
                            ]
                            value = jnp.where(live, value, 0.0)
                            normed = (value - mean_here) * rstd
                            z = scale * normed + shift
                            square = z * z
                            bent = jnp.tanh(z * (slope + (slope * cubic) * square))
                            half = 0.5 + 0.5 * bent
                            abuf[spot, here, lanes] = jnp.where(live, z * half, 0.0)
                            back = half + z * (1.0 - bent * bent) * (
                                0.5 * slope + (1.5 * slope * cubic) * square
                            )
                            grad = jnp.where(live, cbuf[spot, here, lanes].astype(f32) * back, 0.0)
                            into = pl.ds(
                                pl.multiple_of((slot + 1) * SLOT + turn * half_slot, half_slot),
                                half_slot,
                            )
                            big[2 + part, into, :] = grad
                            tall = (half_slot // 8, 8, LANE)
                            sums[0, :, lanes] += jnp.sum((grad * normed).reshape(tall), 0)
                            sums[1, :, lanes] += jnp.sum(grad.reshape(tall), 0)

                loop(0, team, one)
                act_copy(g).start()

            loop(0, groups, act_group)
            sbuf[2 * b + 1] = jnp.zeros((8, wide), f32)
            sbuf[2 * b + 1, 0:1, :] = jnp.sum(sums[0], 0, keepdims=True)
            sbuf[2 * b + 1, 1:2, :] = jnp.sum(sums[1], 0, keepdims=True)
            exchange_block(2 * b + 1)
            by_gain, by_bias = (row_of(2 * b + 1, line) for line in (0, 1))
            by_gain = sum(by_gain[1:], by_gain[0])
            by_bias = sum(by_bias[1:], by_bias[0])
            fullest = numbers[0]
            for number in numbers[1:]:
                fullest = jnp.maximum(fullest, number)
            tot_ref[2:3, columns] = fullest
            tot_ref[0:1, columns] = by_gain
            tot_ref[1:2, columns] = by_bias
            norm[2:3, :] = by_gain / count
            norm[3:4, :] = by_bias / count
            act_copy(groups - 2).wait()
            act_copy(groups - 1).wait()

            def grad_tile(t):
                send_partial(b, t).wait_send()
                for step in range(3):
                    block = t * 3 + step
                    pick = picked_rows(block)
                    here = pl.ds(pl.multiple_of(block * SLOT, SLOT), SLOT)
                    live = lax.broadcasted_iota(i32, (SLOT, LANE), 0) < total - block * SLOT
                    for part in range(2):
                        lanes = slice(part * LANE, (part + 1) * LANE)
                        rstd = norm[1:2, lanes]
                        normed = (big[part, here, :] - norm[0:1, lanes]) * rstd
                        value = (rstd * gain_ref[2 * b + part]) * (
                            pick(2 + part) - norm[3:4, lanes] - normed * norm[2:3, lanes]
                        )
                        stage[2 * b + part, here, :] = jnp.where(live, value, 0.0).astype(bf16)
                send_grad(b, t).start()
                give_grad(b, t).start()

            loop(0, turns, grad_tile)
            if b == 1:
                loop(0, turns, lambda t: send_grad(2, t).start())

        def weight_part(source, qs, low, high, fresh):
            some = pl.ds(low * tile, (high - low) * tile)
            left = jnp.concatenate([source[q, some, :] for q in qs], 1)
            width = LANE * len(qs)
            for number, half in enumerate((own, sib)):
                into = slice(number * fw, (number + 1) * fw)
                value = dot(left, half[some, :], 0, 0)
                if fresh:
                    wacc[:width, into] = value
                else:
                    wacc[:width, into] += value

        def share_of(p, kind):
            return (stg_a, rs_a, ag_a, kind) if p == 0 else (stg_b, rs_b, ag_b, 2 * p - 2 + kind)

        def store_shares(p, kind, line):
            stg, _, _, k = share_of(p, kind)
            width = sizes[p] * LANE
            per = fw // LANE
            for number in range(2):
                base = (side if number == 0 else 1 - side) * per
                for step in range(per):
                    lanes = slice(number * fw + step * LANE, number * fw + (step + 1) * LANE)
                    stg[k, base + step] = wacc[line : line + width, lanes].astype(bf16)

        def scatter(p, kind):
            stg, rs, _, k = share_of(p, kind)
            index = (2 * p + kind) * nodes
            return [
                remote(
                    stg.at[k, (me + step) % nodes],
                    rs.at[k, step],
                    r_s.at[index + step],
                    r_r.at[index + step],
                    node_id(step),
                )
                for step in range(1, nodes)
            ]

        def begin(copies):
            for copy in copies:
                copy.start()

        def finish(copies):
            for copy in copies:
                copy.wait()

        def hop(p):
            src, dst = (hop_a, hop_a) if p == 0 else (hop_b, hop_b)
            k = 0 if p == 0 else 2 * p - 2
            return remote(src.at[k], dst.at[k + 1], h_s.at[p], h_r.at[p], peer_id)

        def spread_share(p, kind):
            if kind == 0:
                _, _, ag, k = share_of(p, 0)
                src = ag.at[k // 2]
            else:
                src = hop_a.at[1] if p == 0 else hop_b.at[2 * p - 1]
            index = (2 * p + kind) * nodes
            which = chip if kind == 0 else 1 - chip
            dst = wag_hbm.at[me, which, :, pl.ds(firsts[p] * LANE, sizes[p] * LANE)]
            copies = [
                remote(src, dst, a_s.at[index + step], a_r.at[index + step], node_id(step))
                for step in range(1, nodes)
            ]
            return copies, pltpu.make_async_copy(src, dst, lsem.at[2 * p + kind])

        def begin_spread(p, kind):
            copies, here = spread_share(p, kind)
            begin(copies)
            here.start()

        def finish_spread(p, kind):
            copies, here = spread_share(p, kind)
            finish(copies)
            here.wait()

        def sum_shares(p, kind):
            finish(scatter(p, kind))
            stg, rs, ag, k = share_of(p, kind)
            value = stg[k, me].astype(f32)
            for step in range(1, nodes):
                value += rs[k, step].astype(f32)
            value = jnp.transpose(value).astype(bf16)
            if kind == 0:
                ag[k // 2] = value
                begin_spread(p, 0)
            else:
                if p == 0:
                    hop_a[0] = value
                else:
                    hop_b[2 * p - 2] = value
                hop(p).start()

        def end_hop(p):
            hop(p).wait()
            begin_spread(p, 1)

        def product(p, t, fresh):
            qs = range(firsts[p], firsts[p] + sizes[p])
            columns = slice(firsts[p] * LANE, (firsts[p] + sizes[p]) * LANE)
            forward_grad(p, t).wait_recv()
            left = jnp.concatenate([ref[q, at(t), :] for ref in (stage, glp, gls, recv) for q in qs], 1)
            right = jnp.concatenate(
                [
                    own_half(wc_ref, columns),
                    own_half(wp_ref, columns),
                    ws_ref[:fw, columns],
                    ws_ref[fw:, columns],
                ],
                1,
            )
            value = dot(left, right, 1, 1)
            for q in range(quarter):
                piece = value[:, q * LANE : (q + 1) * LANE]
                if fresh:
                    big[q, at(t), :] = piece
                else:
                    big[q, at(t), :] += piece

        norm_block(0)
        send_weights(0).wait()
        send_weights(1).wait()
        for low, high in ranges:
            weight_part(stage, (0, 1), low, high, low == 0)
        store_shares(0, 0, 0)
        begin(scatter(0, 0))
        norm_block(1)
        for low, high in ranges:
            weight_part(stage, (2, 3), low, high, low == 0)
        store_shares(1, 0, 0)
        store_shares(2, 0, LANE)
        begin(scatter(1, 0))
        begin(scatter(2, 0))
        sum_shares(0, 0)
        pl.semaphore_wait(credit, 1)

        def pass_on(p, t):
            send_grad(p, t).wait_recv()
            forward_grad(p, t).start()

        for low, high in ranges:
            loop(low, high, lambda t: pass_on(0, t))
            weight_part(glp, (0, 1), low, high, low == 0)
        store_shares(0, 1, 0)
        begin(scatter(0, 1))

        def first_product(t):
            give_grad(0, t).wait_recv()
            give_grad(1, t).wait_recv()
            product(0, t, True)

        loop(0, turns, first_product)
        sum_shares(1, 0)
        sum_shares(2, 0)
        sum_shares(0, 1)
        for low, high in ranges:
            loop(low, high, lambda t: pass_on(1, t))
            weight_part(glp, (2,), low, high, low == 0)
        store_shares(1, 1, 0)
        begin(scatter(1, 1))
        loop(0, turns, lambda t: product(1, t, False))
        end_hop(0)
        sum_shares(1, 1)

        def last_turn(t):
            pass_on(2, t)

            @pl.when(t >= 2)
            def _():
                product(2, t - 2, False)

        for low, high in ranges:
            loop(low, high, last_turn)
            weight_part(glp, (3,), low, high, low == 0)
        store_shares(2, 1, 0)
        begin(scatter(2, 1))
        for t in (turns - 2, turns - 1):
            product(2, t, False)
        end_hop(1)

        def link_copy(g):
            return pltpu.make_async_copy(
                tile_hbm.at[pl.ds(g * team, team), pl.ds(SLOT, 2 * SLOT)],
                tbuf.at[g % 3, :, pl.ds(SLOT, 2 * SLOT)],
                tsem.at[g % 3],
            )

        def slot_copy(g):
            return pltpu.make_async_copy(
                gbuf.at[g % 2],
                slot_hbm.at[pl.ds(pl.multiple_of(g * team * SLOT, SLOT), team * SLOT)],
                gsem.at[g % 2],
            )

        link_copy(0).start()
        link_copy(1).start()
        link_total[...] = jnp.zeros_like(link_total)
        place_row = lax.broadcasted_iota(i32, (SLOT, LANE), 0)

        def slot_group(g):
            @pl.when(g + 2 < groups)
            def _():
                link_copy(g + 2).start()

            link_copy(g).wait()

            @pl.when(g >= 2)
            def _():
                slot_copy(g - 2).wait()

            for member in range(team):
                slot = g * team + member
                live = place_row < cnt_ref[slot]
                scale = column_of(inv_ref, slot)
                for q in range(quarter):
                    value = big[q, pl.ds(off_ref[slot], SLOT), :].astype(bf16).astype(f32)
                    gbuf[g % 2, member * SLOT : (member + 1) * SLOT, q * LANE : (q + 1) * LANE] = (
                        jnp.where(live, value * scale, 0.0).astype(bf16)
                    )
            link = jnp.concatenate([tbuf[g % 3, member, SLOT:, :] for member in range(team)], 1)
            link_total[...] += dot(link, gbuf[g % 2])
            slot_copy(g).start()

        loop(0, groups, slot_group)
        hbuf[...] = link_total[...].astype(bf16)
        half = hbuf.shape[0] // 2
        returns = [
            remote(hbuf.at[:half], hback.at[:half], b_s.at[0], b_r.at[0], node_id(nodes - 1)),
            remote(hbuf.at[half:], hback.at[half:], b_s.at[1], b_r.at[1], node_id(1)),
        ]
        begin(returns)
        sum_shares(2, 1)
        slot_copy(groups - 2).wait()
        slot_copy(groups - 1).wait()
        finish(returns)
        back_ref[:half, :] = jnp.where(me == nodes - 1, 0.0, hback[:half, :].astype(f32)).astype(bf16)
        back_ref[half:, :] = jnp.where(me == 0, 0.0, hback[half:, :].astype(f32)).astype(bf16)
        end_hop(2)

        def settle(t):
            send_own(t).wait_send()
            for b in range(2):
                give_grad(b, t).wait_send()
            for p in range(3):
                send_grad(p, t).wait_send()
                forward_grad(p, t).wait_send()

        loop(0, turns, settle)
        for p in range(3):
            for kind in range(2):
                finish_spread(p, kind)

    anywhere = pl.BlockSpec(memory_space=pl.ANY)
    dma = pltpu.SemaphoreType.DMA
    lane_rows = (quarter, compact, LANE)
    outs = [
        jax.ShapeDtypeStruct((rows, fw), f32),
        jax.ShapeDtypeStruct((rows, fw), bf16),
        jax.ShapeDtypeStruct((2 * SLOT, fw), bf16),
        jax.ShapeDtypeStruct((nodes, 2, LANE, fw), bf16),
        jax.ShapeDtypeStruct((8, fw), f32),
        jax.ShapeDtypeStruct((slots, 3 * SLOT, SLOT), bf16),
    ]
    scratch = [
        pltpu.VMEM((compact, fw), bf16),
        pltpu.VMEM((compact, fw), bf16),
        pltpu.VMEM(lane_rows, bf16),
        pltpu.VMEM(lane_rows, bf16),
        pltpu.VMEM(lane_rows, bf16),
        pltpu.VMEM(lane_rows, bf16),
        pltpu.VMEM((quarter, padded, LANE), f32),
        pltpu.VMEM((wide, 2 * fw), f32),
        pltpu.VMEM((2, nodes, wide, LANE), bf16),
        pltpu.VMEM((4, nodes, LANE, LANE), bf16),
        pltpu.VMEM((2, nodes, wide, LANE), bf16),
        pltpu.VMEM((4, nodes, LANE, LANE), bf16),
        pltpu.VMEM((1, LANE, wide), bf16),
        pltpu.VMEM((2, LANE, LANE), bf16),
        pltpu.VMEM((2, LANE, wide), bf16),
        pltpu.VMEM((4, LANE, LANE), bf16),
        pltpu.VMEM((3, team * SLOT, fw), bf16),
        pltpu.VMEM((3, team, 3 * SLOT, SLOT), bf16),
        pltpu.VMEM((2, team * SLOT, wide), bf16),
        pltpu.VMEM((2, team * SLOT, wide), f32),
        pltpu.VMEM((2, team * SLOT, fw), bf16),
        pltpu.VMEM((4, 8, wide), f32),
        pltpu.VMEM((4, nodes, 8, wide), f32),
        pltpu.VMEM((8, wide), f32),
        pltpu.VMEM((2, 8, wide), f32),
        pltpu.VMEM((8, wide), f32),
        pltpu.VMEM((2 * SLOT, fw), f32),
        pltpu.VMEM((2 * SLOT, fw), bf16),
        pltpu.VMEM((2 * SLOT, fw), bf16),
        dma((3,)),
        dma((3,)),
        dma((2,)),
        dma((2,)),
        dma((2,)),
        dma((turns,)),
        dma((turns,)),
        dma((2 * turns,)),
        dma((2 * turns,)),
        dma((3 * turns,)),
        dma((3 * turns,)),
        dma((2 * turns,)),
        dma((2 * turns,)),
        dma((3 * turns,)),
        dma((3 * turns,)),
        dma((4 * nodes,)),
        dma((4 * nodes,)),
        dma((6 * nodes,)),
        dma((6 * nodes,)),
        dma((3,)),
        dma((3,)),
        dma((6 * nodes,)),
        dma((6 * nodes,)),
        dma((4,)),
        dma((4,)),
        dma((6,)),
        pltpu.SemaphoreType.REGULAR,
        pltpu.VMEM((2 * fw, fw), bf16),
        dma((2,)),
        dma((2,)),
        pltpu.VMEM((2 * fw, fw), bf16),
        pltpu.VMEM((2 * fw, fw), bf16),
        dma((2 * quarter,)),
        dma((4,)),
        dma((4,)),
        pltpu.VMEM((2 * SLOT, fw), bf16),
        pltpu.VMEM((slots, 8, SLOT), f32),
    ]
    return pl.pallas_call(
        kernel,
        out_shape=outs,
        in_specs=[smem()] * 3 + [anywhere] * 3 + [whole()] * 5,
        out_specs=[anywhere, anywhere, whole(), anywhere, whole(), anywhere],
        scratch_shapes=scratch,
        compiler_params=pltpu.CompilerParams(
            vmem_limit_bytes=CORE_BYTES, collective_id=2, has_side_effects=True
        ),
        cost_estimate=cost(0, 0),
        name="core",
    )(*lists, features, weight, cotangent, near, links, send_row, gain, bias)


def every_row(
    features, weight, cotangent, near, links, send_list, valid_row, scale, shift, lists, nodes, chips
):
    offsets, counts = lists[:2]
    rows, fw = features.shape
    slots = rows // SLOT
    chip, core_side = lax.axis_index("mp") // 2, lax.rem(lax.axis_index("mp"), 2)
    core_word = core_side.astype(i32)[None]
    half = send_list.shape[0] // 2
    others = range(1, chips)
    wide = fw // 2

    def chip_rows(which):
        return lax.dynamic_slice_in_dim(weight, which * 2 * fw, 2 * fw, 0).astype(bf16)

    w_peer = [to_chip(chip_rows(lax.rem(chip + d, chips)), d) for d in others]
    w_chip = chip_rows(chip)
    picked = pick_rows(features, send_list[:, None], valid_row)
    halo = jnp.concatenate([node_shift(picked[:half], 1), node_shift(picked[half:], -1)], 0)
    tiles, inv = count_tiles(near, links, counts)

    def half_of(block, which):
        return lax.dynamic_slice_in_dim(block, which * fw, fw, 0)

    w_all = [w_chip] + w_peer
    got = to_sibling(jnp.concatenate([half_of(w, 1 - core_side) for w in w_all], 0))
    wb = [half_of(w, core_side) for w in w_all] + [got[i * fw : (i + 1) * fw] for i in range(chips)]
    own = aggregate(tiles, inv, features, halo, offsets, counts, 0, rows)
    sib = to_sibling(own)
    received = []
    for b in range(2):
        parts = [partial_product(own, sib, w, core_word, b, wide) for w in w_peer]
        received.append([to_chip(p, -d) for p, d in zip(parts, others, strict=True)])
    gain, bias = scale[None, :], shift[None, :]
    act, grads, totals, weight_grads = None, [], [], []
    for b in range(2):
        lin, stat = linear_stats(
            own, sib, w_chip, core_word, received[b], offsets, slots, b, wide
        )
        stats = exchange(stat, nodes)
        act, grad_pre, sums = activate(
            lin, stats, gain, bias, cotangent, offsets, counts, act, b, wide, rows, fw
        )
        sums = exchange(sums, nodes)
        grad_lin, summed = linear_grad(
            lin, grad_pre, stats, sums, gain, offsets, slots, b, wide, 1
        )
        totals.append(summed)
        mine = [grad_lin] + [to_chip(grad_lin, d) for d in others]
        grads.append(mine + [to_sibling(g) for g in mine])
        sets = []
        for g in mine:
            left = jnp.einsum("rf,rc->fc", own, g, preferred_element_type=f32)
            right = jnp.einsum("rf,rc->fc", sib, g, preferred_element_type=f32)
            sets.append(
                jnp.concatenate(
                    [
                        jnp.where(core_side == 1, right, left),
                        jnp.where(core_side == 1, left, right),
                    ],
                    0,
                )
            )
        share = scatter_sum(jnp.stack(sets), 1)
        shares = [share[0]] + [to_chip(share[d], -d) for d in others]
        full = gather_shares(jnp.stack(shares), 1)
        placed = jnp.zeros((chips,) + full.shape[1:], f32)
        for d in range(chips):
            placed = lax.dynamic_update_slice(
                placed, full[d : d + 1], (lax.rem(chip + d, chips), 0, 0)
            )
        weight_grads.append(placed.reshape(chips * 2 * fw, wide))
    grad_agg = grad_products(grads[0], wb, [0] * len(wb))
    slot_grad, halo_grad = slot_grads(grad_agg, grads[1], wb, wide, tiles, inv, offsets, counts)
    returned = jnp.concatenate(
        [node_shift(halo_grad[:half], -1), node_shift(halo_grad[half:], 1)], 0
    )
    input_grad = input_grads(slot_grad, tiles, returned, send_list[None, :], counts)
    totals = jnp.concatenate(totals, 1)
    return act, input_grad, jnp.concatenate(weight_grads, 1), totals[0], totals[1]


def local(features, weight, scale, shift, cotangent, neighbours, halo_links, valid_rows, send_rows):
    rows, fw = features.shape
    slots = rows // SLOT
    nodes, mp = lax.axis_size("node"), lax.axis_size("mp")
    chips = mp // 2

    counts = jnp.sum(valid_rows.reshape(slots, SLOT), 1).astype(i32)
    order = jnp.arange(slots + 1, dtype=i32)
    offsets = jnp.sum(jnp.where(order[None, :slots] < order[:, None], counts[None, :], 0), 1)
    compact = rows * 13 // 16 // (3 * SLOT) * (3 * SLOT)
    blocks = jnp.arange(compact // SLOT, dtype=i32) * SLOT
    first = jnp.minimum(
        jnp.sum((offsets[None, 1:] <= blocks[:, None]).astype(i32), 1), slots - 1
    ).astype(i32)
    lists = (offsets, counts, first)
    near, links = neighbours.T, halo_links.T
    send_list = jnp.concatenate([send_rows[:, 1], send_rows[:, 0]], 0)
    valid_row = valid_rows[None, :].astype(i32)

    def all_rows(*args):
        return every_row(*args, lists, nodes, chips)

    given = (features, weight, cotangent, near, links, send_list, valid_row, scale, shift)
    if not (chips == 2 and fw == 4 * LANE and 2 * fw == nodes * LANE and slots % nodes == 0):
        return all_rows(*given)
    send_row = send_list[None, :]
    *made, totals, tiles = core(
        features, weight, cotangent, near, links, send_row, scale, shift, lists, nodes, compact
    )

    def few_rows(*args):
        act, input_grad, weight_grad = last_pass(*made, tiles, send_row, counts)
        return act, input_grad, weight_grad.reshape(mp * fw, fw), totals[0], totals[1]

    return lax.cond(totals[2, 0] <= compact, few_rows, all_rows, *given)


def solution(mesh):
    in_specs = (
        P("node", "mp"),
        P(None, "mp"),
        P("mp"),
        P("mp"),
        P("node", "mp"),
        P("node", None),
        P("node", None),
        P("node"),
        P("node", None),
    )
    out_specs = (P("node", "mp"), P("node", "mp"), P(None, "mp"), P("mp"), P("mp"))
    return jax.shard_map(local, mesh=mesh, in_specs=in_specs, out_specs=out_specs, check_vma=False)
```

profile of v0, /device:TPU:0, one launch (start us, length us, event | category | flops | bytes accessed | tf_op | source)
XLA Modules:
  0.0 316.4 jit_solution(11381101229236749360)
XLA Ops:
  0.6 0.8 bitcast_reduce_fusion.refs_1_
  1.5 0.1 select_reduce_fusion.refs_0_
  1.6 0.1 slice.70
  1.7 0.2 convert_reduce_fusion
  1.8 0.5 broadcast_minimum_fusion.refs_2_
  2.4 0.8 slice_bitcast_fusion.3
  3.1 0.0 copy-start.17
  3.1 0.0 copy-start.21
  3.2 0.0 copy-start.23
  3.2 0.0 copy-start.24
  3.2 0.0 copy-start.25
  3.2 290.2 %core.1 = (f32[6144,512]{1,0:T(8,128)}, bf16[6144,512]{1,0:T(8,128)(2,1)}, bf16[256,512]{1,0:T(8,128)(2,1)}, bf16[8,2,128,512]{3,2,1,0:T(8,128)(2,1)}, f32[8,512...) custom-call(s32[49]{0:T(128)S(1)} %select_reduce_fusion.refs_0_, s32[48]{0:T(128)S(1)} %bitcast_reduce_fusion.refs_1_, ...), custom_call_target="tpu_custom_call" | custom-call | flops 1 | bytes 1 | tf_op jit(solution)/shard_map/core/pallas_call | solution.py:1678
  293.4 0.5 slice.73
  294.5 0.0 copy-done.17
  294.6 0.0 copy-done.21
  294.6 0.0 copy-done.23
  294.6 0.0 copy-done.24
  294.6 0.0 copy-done.25
  294.6 21.8 %conditional.1 = (f32[6144,512]{1,0:T(8,128)}, f32[6144,512]{1,0:T(8,128)}, f32[2048,512]{1,0:T(8,128)}, f32[512]{0:T(512)}, f32[512]{0:T(512)}) conditional(s32[]{:T(128)} %bitcast.29, (s32[48]{0:T(128)S(1)}, s32[16,6144]{1,0:T(8,128)S(1)}, s32[4,6144]{1,0:T(4,128)S(1)}, s32[256]{0:T(256)S(1)}, bf16[6144,512]{1,0:T(8,128)(2,1)}, ...), branch_computations={%region_3.4_spmd, %region_4.5_spmd} | conditional | flops 12897878016 | bytes 500249184 | solution.py:1808
  294.9 20.9 %last_pass.1 = (f32[6144,512]{1,0:T(8,128)}, f32[6144,512]{1,0:T(8,128)}, f32[2,8,128,512]{3,2,1,0:T(8,128)}) custom-call(s32[48]{0:T(128)S(1)} %get-tuple-element.67.counts_ref, f32[6144,512]{1,0:T(8,128)} %get-tuple-element.68.act_ref, bf16[6144,512]{1,0:T(8,128)(2,1)} %get-tuple-element.69.grad_ref, bf16[48,384,128]{2,1,0:T(8,128)(2,1)} %get-tuple-element.70.tile_ref, ...), custom_call_target="tpu_custom_call" | custom-call | flops 1 | bytes 1 | tf_op jit(solution)/shard_map/cond/branch_1_fun/last_pass/pallas_call | solution.py:746
  315.8 0.6 fusion.12
  (3 shorter events, 0.0 us)
Async XLA Ops:
  3.1 291.4 %copy-start.17 = (s32[6144,16]{0,1:T(8,128)S(1)}, s32[6144,16]{0,1:T(8,128)}, u32[]{:S(2)}) copy-start(s32[6144,16]{0,1:T(8,128)} %param.16) | copy-start | bytes 1179652
  3.1 291.4 %copy-start.21 = (s32[6144,4]{0,1:T(4,128)S(1)}, s32[6144,4]{0,1:T(4,128)}, u32[]{:S(2)}) copy-start(s32[6144,4]{0,1:T(4,128)} %param.17) | copy-start | bytes 294916
  3.2 291.4 %copy-start.23 = (s32[6144]{0:T(1024)S(1)}, s32[6144]{0:T(1024)}, u32[]{:S(2)}) copy-start(s32[6144]{0:T(1024)} %param.18) | copy-start | bytes 73732
  3.2 291.4 %copy-start.24 = (f32[512]{0:T(512)S(1)}, f32[512]{0:T(512)}, u32[]{:S(2)}) copy-start(f32[512]{0:T(512)} %param.13) | copy-start | bytes 6148
  3.2 291.4 %copy-start.25 = (f32[512]{0:T(512)S(1)}, f32[512]{0:T(512)}, u32[]{:S(2)}) copy-start(f32[512]{0:T(512)} %param.14) | copy-start | bytes 6148
where the time goes:
time: 317 us; the launch traced here: 316 us
  Pallas kernels  311 us (98%)
    pallas_call x1, Pallas kernels, core(): pl.pallas_call(kernel, out_shape=outs, in_specs=[smem()] * 3 + [anywhere]...  290 us
    pallas_call x1, Pallas kernels, last_pass(): pl.pallas_call(kernel, grid=(nodes,), out_shape=[jax.ShapeDtypeStruct((ro...  20.9 us

commit v1 on v0

--- a/solution.py
+++ b/solution.py
@@ -829,7 +829,8 @@
     wide = fw // 2
     team = 4
     groups = slots // team
-    ranges = [(0, 4), (4, 8), (8, turns)]
+    ranges = [(0, 5), (5, 10), (10, turns)]
+    early = 2
     slope, cubic = 0.7978845608028654, 0.044715
     sizes = {0: 2, 1: 1, 2: 1}
     firsts = {0: 0, 1: 2, 2: 3}
@@ -843,8 +844,9 @@
         fbuf, tbuf, cbuf, abuf, gbuf, sbuf, ebuf, st, sums, norm, link_total, hbuf, hback = refs[33:46]
         fsem, tsem, csem, asem, gsem = refs[46:51]
         d1s, d1r, x1s, x1r, x2s, x2r, d2s, d2r, f2s, f2r = refs[51:61]
-        e_s, e_r, r_s, r_r, h_s, h_r, a_s, a_r, b_s, b_r, lsem, credit = refs[61:73]
-        ws_ref, w_s, w_r, wc_ref, wp_ref, wsem, v_s, v_r, halo_ref, inv_ref = refs[73:83]
+        e_s, e_r, r_s, r_r, a_s, a_r, b_s, b_r, lsem, credit = refs[61:71]
+        ws_ref, w_s, w_r, wc_ref, wp_ref, wsem, v_s, v_r, halo_ref, inv_ref = refs[71:81]
+        u_s, u_r, h_s, h_r = refs[81:85]
 
         me = lax.axis_index("node")
         place = lax.axis_index("mp")
@@ -855,6 +857,9 @@
 
         def node_id(step):
             return {"node": (me + step) % nodes}
+
+        def across_id(step):
+            return {"node": (me + step) % nodes, "mp": (1 - chip) * 2 + side}
 
         def weight_copy(mine, q):
             chosen_rows = chip if mine else 1 - chip
@@ -871,7 +876,8 @@
             for q in range(quarter):
                 weight_copy(mine, q).start()
         barrier = pltpu.get_barrier_semaphore()
-        for target in [peer_id, sib_id] + [node_id(step) for step in range(1, nodes)]:
+        targets = [sib_id] + [node_id(step) for step in range(1, nodes)]
+        for target in targets + [across_id(step) for step in range(nodes)]:
             pl.semaphore_signal(barrier, inc=1, device_id=target, device_id_type=MESH)
 
         def remote(src, dst, send, arrive, target):
@@ -900,38 +906,37 @@
 
             lax.fori_loop(low, high, step, 0)
 
-        def send_own(t):
-            return remote(own.at[at(t)], sib.at[at(t)], d1s.at[t], d1r.at[t], sib_id)
-
-        def send_partial(b, t):
+        def span(low, high):
+            return pl.ds(pl.multiple_of(low * tile, SLOT), (high - low) * tile)
+
+        every = span(0, turns)
+
+        def send_own(t, rows_of=None):
+            here = at(t) if rows_of is None else rows_of
+            return remote(
+                own.at[here], sib.at[here], d1s.at[0], d1r.at[0 if rows_of else t], sib_id
+            )
+
+        def send_partial(b, part, here):
             two = pl.ds(2 * b, 2)
             return remote(
-                stage.at[two, at(t)],
-                recv.at[two, at(t)],
-                x1s.at[b * turns + t],
-                x1r.at[b * turns + t],
-                peer_id,
-            )
-
-        def send_grad(p, t):
+                stage.at[two, here], recv.at[two, here], x1s.at[b], x1r.at[3 * b + part], peer_id
+            )
+
+        def send_grad(p, part, here):
             some = pl.ds(firsts[p], sizes[p])
-            index = p * turns + t
             return remote(
-                stage.at[some, at(t)], glp.at[some, at(t)], x2s.at[index], x2r.at[index], peer_id
-            )
-
-        def give_grad(b, t):
+                stage.at[some, here], glp.at[some, here], x2s.at[p], x2r.at[3 * p + part], peer_id
+            )
+
+        def give_grad(b, here):
             two = pl.ds(2 * b, 2)
-            index = b * turns + t
+            return remote(stage.at[two, here], gls.at[two, here], d2s.at[b], d2r.at[b], sib_id)
+
+        def forward_grad(p, part, here):
+            some = pl.ds(firsts[p], sizes[p])
             return remote(
-                stage.at[two, at(t)], gls.at[two, at(t)], d2s.at[index], d2r.at[index], sib_id
-            )
-
-        def forward_grad(p, t):
-            some = pl.ds(firsts[p], sizes[p])
-            index = p * turns + t
-            return remote(
-                glp.at[some, at(t)], recv.at[some, at(t)], f2s.at[index], f2r.at[index], sib_id
+                glp.at[some, here], recv.at[some, here], f2s.at[p], f2r.at[p + part], sib_id
             )
 
         def picked_rows(block):
@@ -965,15 +970,39 @@
                 sib_id,
             )
 
-        def send_peer_weights(half, number):
-            columns = pl.ds(half * wide, wide)
+        first_half, second_half = slice(0, wide), slice(wide, fw)
+
+        def send_upper_weights():
+            columns = pl.ds(0, wide)
             return remote(
-                gbuf.at[number, :, columns],
-                wp_ref.at[pl.ds(number * fw, fw), columns],
-                v_s.at[2 * half + number],
-                v_r.at[2 * half + number],
-                peer_id,
-            )
+                gbuf.at[0, :, columns], wp_ref.at[pl.ds(0, fw), columns], v_s.at[2], v_r.at[2], peer_id
+            )
+
+        per_half = nodes // 2
+
+        def share_of_weights(which):
+            if which == 0:
+                start = pl.multiple_of(me * (LANE // 2), LANE // 2)
+                source = gbuf.at[1, pl.ds(start, LANE // 2), pl.ds(0, wide)]
+                return source, wp_ref.at[pl.ds(fw + start, LANE // 2), pl.ds(0, wide)]
+            start = pl.multiple_of((me % per_half) * LANE, LANE)
+            source = gbuf.at[me // per_half, pl.ds(start, LANE), pl.ds(wide, wide)]
+            into = pl.ds(pl.multiple_of(me * LANE, LANE), LANE)
+            return source, wp_ref.at[into, pl.ds(wide, wide)]
+
+        def send_weight_share(which):
+            source, into = share_of_weights(which)
+            return remote(source, into, v_s.at[which], v_r.at[which], peer_id)
+
+        def spread_weights(which):
+            _, into = share_of_weights(which)
+            for step in range(1, nodes):
+                remote(into, into, u_s.at[which], u_r.at[which], node_id(step)).start()
+
+        def spread_weights_end(which):
+            count = (nodes - 1) * (LANE // 2 if which == 0 else LANE)
+            some = wp_ref.at[pl.ds(0, count), pl.ds(which * wide, wide)]
+            return remote(some, some, u_s.at[which], u_r.at[which], node_id(1))
 
         def loads(g):
             return pltpu.make_async_copy(
@@ -989,14 +1018,6 @@
             weight_copy(0, q).wait()
             for number in range(2):
                 gbuf[number, :, lanes] = big[q, number * fw : (number + 1) * fw, :].astype(bf16)
-        pl.semaphore_wait(barrier, nodes + 1)
-        for half in range(2):
-            for number in range(2):
-                send_peer_weights(half, number).start()
-        for q in range(quarter):
-            weight_copy(1, q).wait()
-            wc_ref[:, q * LANE : (q + 1) * LANE] = big[q, 2 * fw : 4 * fw, :].astype(bf16)
-
         wanted = [
             jnp.transpose(
                 jnp.broadcast_to(
@@ -1037,8 +1058,15 @@
                 node_id(nodes - 1),
             ),
         ]
+        pl.semaphore_wait(barrier, 2 * nodes)
+        send_weight_share(0).start()
+        send_upper_weights().start()
+        send_weight_share(1).start()
         for copy in halo_in:
             copy.start()
+        for q in range(quarter):
+            weight_copy(1, q).wait()
+            wc_ref[:, q * LANE : (q + 1) * LANE] = big[q, 2 * fw : 4 * fw, :].astype(bf16)
         for g in range(2):
             loads(g).start()
 
@@ -1046,7 +1074,6 @@
         column = lax.broadcasted_iota(i32, (SLOT, SLOT), 1)
         link_row = lax.broadcasted_iota(i32, (2 * SLOT, SLOT), 0)
         unit = jnp.where(row == column, 1.0, 0.0).astype(bf16)
-        first_half, second_half = slice(0, wide), slice(wide, fw)
 
         def tile_copy(g):
             return pltpu.make_async_copy(
@@ -1078,6 +1105,8 @@
             loop(0, team, one)
             tile_copy(g).start()
 
+        send_weight_share(0).wait_recv()
+        spread_weights(0)
         count_group(0)
         count_group(1)
         for copy in halo_in:
@@ -1090,14 +1119,13 @@
         ).astype(bf16)
 
         def partial(b, t):
+            part = jnp.where(t < ranges[0][1], 0, jnp.where(t < ranges[1][1], 1, 2))
             columns = second_half if b else first_half
             value = dot(own[at(t), :], own_half(wp_ref, columns))
             value += dot(sib[at(t), :], sib_half(wp_ref, columns))
-            for part in range(2):
-                stage[2 * b + part, at(t), :] = value[:, part * LANE : (part + 1) * LANE].astype(
-                    bf16
-                )
-            send_partial(b, t).start()
+            for q in range(2):
+                stage[2 * b + q, at(t), :] = value[:, q * LANE : (q + 1) * LANE].astype(bf16)
+            send_partial(b, part, at(t)).start()
 
         def first_partial(t):
             send_own(t).wait_recv()
@@ -1114,8 +1142,10 @@
 
             @pl.when(t == 1)
             def _():
-                for number in range(2):
-                    send_peer_weights(0, number).wait_recv()
+                send_weight_share(1).wait_recv()
+                spread_weights(1)
+                send_upper_weights().wait_recv()
+                spread_weights_end(0).wait_recv()
 
             @pl.when(t >= 1)
             def _():
@@ -1151,32 +1181,29 @@
 
         loop(0, groups, gather_group)
         first_partial(turns - 1)
-        for number in range(2):
-            send_peer_weights(1, number).wait_recv()
+        spread_weights_end(1).wait_recv()
         loop(0, turns, lambda t: partial(1, t))
         send_weights(0).start()
         send_weights(1).start()
-        for half in range(2):
-            for number in range(2):
-                send_peer_weights(half, number).wait_send()
+        send_upper_weights().wait_send()
+        for which in range(2):
+            send_weight_share(which).wait_send()
+            spread_weights_end(which).wait_send()
         for g in range(groups - 3, groups):
             tile_copy(g).wait()
 
         def exchange_block(number):
-            copies = []
             for step in range(1, nodes):
-                copy = remote(
+                remote(
                     sbuf.at[number],
                     ebuf.at[number, step],
-                    e_s.at[number * nodes + step],
-                    e_r.at[number * nodes + step],
+                    e_s.at[number],
+                    e_r.at[number],
                     node_id(step),
-                )
-                copy.start()
-                copies.append(copy)
+                ).start()
             ebuf[number, 0] = sbuf[number]
-            for copy in copies:
-                copy.wait()
+            others = ebuf.at[number, pl.ds(1, nodes - 1)]
+            remote(others, others, e_s.at[number], e_r.at[number], node_id(1)).wait()
 
         def row_of(number, line):
             return [ebuf[number, node, line : line + 1, :] for node in range(nodes)]
@@ -1186,7 +1213,6 @@
             st[...] = jnp.zeros_like(st)
 
             def linear_tile(t):
-                send_partial(b, t).wait_recv()
                 value = dot(own[at(t), :], own_half(wc_ref, columns))
                 value += dot(sib[at(t), :], sib_half(wc_ref, columns))
                 begin = t * tile
@@ -1210,7 +1236,9 @@
                     st[0:1, lanes] = mean + gap * ratio
                     st[1:2, lanes] = held + squares + gap * gap * (seen * ratio)
 
-            loop(0, turns, linear_tile)
+            for part, (low, high) in enumerate(ranges):
+                send_partial(b, part, span(low, high)).wait_recv()
+                loop(low, high, linear_tile)
             if b == 1:
                 pl.semaphore_signal(credit, inc=1, device_id=sib_id, device_id_type=MESH)
             st[2:3, :] = jnp.full((1, wide), total.astype(f32), f32)
@@ -1322,7 +1350,6 @@
             act_copy(groups - 1).wait()
 
             def grad_tile(t):
-                send_partial(b, t).wait_send()
                 for step in range(3):
                     block = t * 3 + step
                     pick = picked_rows(block)
@@ -1336,12 +1363,15 @@
                             pick(2 + part) - norm[3:4, lanes] - normed * norm[2:3, lanes]
                         )
                         stage[2 * b + part, here, :] = jnp.where(live, value, 0.0).astype(bf16)
-                send_grad(b, t).start()
-                give_grad(b, t).start()
-
-            loop(0, turns, grad_tile)
+                give_grad(b, at(t)).start()
+                send_grad(b, part_number[0], at(t)).start()
+
+            send_partial(b, 0, every).wait_send()
+            for part, (low, high) in enumerate(ranges):
+                part_number = [part]
+                loop(low, high, grad_tile)
             if b == 1:
-                loop(0, turns, lambda t: send_grad(2, t).start())
+                loop(0, early, lambda t: send_grad(2, t, at(t)).start())
 
         def weight_part(source, qs, low, high, fresh):
             some = pl.ds(low * tile, (high - low) * tile)
@@ -1368,19 +1398,29 @@
                     lanes = slice(number * fw + step * LANE, number * fw + (step + 1) * LANE)
                     stg[k, base + step] = wacc[line : line + width, lanes].astype(bf16)
 
+        def crosses(p, kind):
+            return kind == 1 and p == 2
+
         def scatter(p, kind):
             stg, rs, _, k = share_of(p, kind)
-            index = (2 * p + kind) * nodes
+            index = 2 * p + kind
             return [
                 remote(
                     stg.at[k, (me + step) % nodes],
                     rs.at[k, step],
-                    r_s.at[index + step],
-                    r_r.at[index + step],
-                    node_id(step),
+                    r_s.at[index],
+                    r_r.at[index],
+                    across_id(step) if crosses(p, kind) else node_id(step),
                 )
-                for step in range(1, nodes)
+                for step in range(0 if crosses(p, kind) else 1, nodes)
             ]
+
+        def scattered(p, kind):
+            _, rs, _, k = share_of(p, kind)
+            first = 0 if crosses(p, kind) else 1
+            shares = rs.at[k, pl.ds(first, nodes - first)]
+            index = 2 * p + kind
+            return remote(shares, shares, r_s.at[index], r_r.at[index], peer_id)
 
         def begin(copies):
             for copy in copies:
@@ -1391,21 +1431,17 @@
                 copy.wait()
 
         def hop(p):
-            src, dst = (hop_a, hop_a) if p == 0 else (hop_b, hop_b)
-            k = 0 if p == 0 else 2 * p - 2
-            return remote(src.at[k], dst.at[k + 1], h_s.at[p], h_r.at[p], peer_id)
+            _, _, ag, k = share_of(p, 1)
+            return remote(hop_b if p else hop_a, ag.at[k], h_s.at[p], h_r.at[p], peer_id)
 
         def spread_share(p, kind):
-            if kind == 0:
-                _, _, ag, k = share_of(p, 0)
-                src = ag.at[k // 2]
-            else:
-                src = hop_a.at[1] if p == 0 else hop_b.at[2 * p - 1]
-            index = (2 * p + kind) * nodes
+            _, _, ag, k = share_of(p, kind)
+            src = ag.at[k]
+            index = 2 * p + kind
             which = chip if kind == 0 else 1 - chip
             dst = wag_hbm.at[me, which, :, pl.ds(firsts[p] * LANE, sizes[p] * LANE)]
             copies = [
-                remote(src, dst, a_s.at[index + step], a_r.at[index + step], node_id(step))
+                remote(src, dst, a_s.at[index], a_r.at[index], node_id(step))
                 for step in range(1, nodes)
             ]
             return copies, pltpu.make_async_copy(src, dst, lsem.at[2 * p + kind])
@@ -1416,26 +1452,27 @@
             here.start()
 
         def finish_spread(p, kind):
-            copies, here = spread_share(p, kind)
-            finish(copies)
+            _, here = spread_share(p, kind)
+            index = 2 * p + kind
+            shares = wag_hbm.at[
+                pl.ds(0, nodes - 1), 0, :, pl.ds(firsts[p] * LANE, sizes[p] * LANE)
+            ]
+            remote(shares, shares, a_s.at[index], a_r.at[index], node_id(1)).wait()
             here.wait()
 
         def sum_shares(p, kind):
-            finish(scatter(p, kind))
+            scattered(p, kind).wait()
             stg, rs, ag, k = share_of(p, kind)
-            value = stg[k, me].astype(f32)
+            value = (rs[k, 0] if crosses(p, kind) else stg[k, me]).astype(f32)
             for step in range(1, nodes):
                 value += rs[k, step].astype(f32)
             value = jnp.transpose(value).astype(bf16)
-            if kind == 0:
-                ag[k // 2] = value
-                begin_spread(p, 0)
+            if kind == 1 and not crosses(p, kind):
+                (hop_b if p else hop_a)[...] = value
+                hop(p).start()
             else:
-                if p == 0:
-                    hop_a[0] = value
-                else:
-                    hop_b[2 * p - 2] = value
-                hop(p).start()
+                ag[k] = value
+                begin_spread(p, kind)
 
         def end_hop(p):
             hop(p).wait()
@@ -1444,7 +1481,6 @@
         def product(p, t, fresh):
             qs = range(firsts[p], firsts[p] + sizes[p])
             columns = slice(firsts[p] * LANE, (firsts[p] + sizes[p]) * LANE)
-            forward_grad(p, t).wait_recv()
             left = jnp.concatenate([ref[q, at(t), :] for ref in (stage, glp, gls, recv) for q in qs], 1)
             right = jnp.concatenate(
                 [
@@ -1470,6 +1506,7 @@
             weight_part(stage, (0, 1), low, high, low == 0)
         store_shares(0, 0, 0)
         begin(scatter(0, 0))
+        sum_shares(0, 0)
         norm_block(1)
         for low, high in ranges:
             weight_part(stage, (2, 3), low, high, low == 0)
@@ -1477,52 +1514,34 @@
         store_shares(2, 0, LANE)
         begin(scatter(1, 0))
         begin(scatter(2, 0))
-        sum_shares(0, 0)
         pl.semaphore_wait(credit, 1)
 
-        def pass_on(p, t):
-            send_grad(p, t).wait_recv()
-            forward_grad(p, t).start()
-
-        for low, high in ranges:
-            loop(low, high, lambda t: pass_on(0, t))
+        def pass_range(p, part, low, high):
+            send_grad(p, part, span(low, high)).wait_recv()
+            forward_grad(p, 0, span(low, high)).start()
+
+        for part, (low, high) in enumerate(ranges):
+            pass_range(0, part, low, high)
             weight_part(glp, (0, 1), low, high, low == 0)
         store_shares(0, 1, 0)
         begin(scatter(0, 1))
-
-        def first_product(t):
-            give_grad(0, t).wait_recv()
-            give_grad(1, t).wait_recv()
-            product(0, t, True)
-
-        loop(0, turns, first_product)
         sum_shares(1, 0)
         sum_shares(2, 0)
+
+        for b in range(2):
+            give_grad(b, every).wait_recv()
+        forward_grad(0, 0, every).wait_recv()
+        loop(0, turns, lambda t: product(0, t, True))
         sum_shares(0, 1)
-        for low, high in ranges:
-            loop(low, high, lambda t: pass_on(1, t))
+        loop(early, turns, lambda t: send_grad(2, t, at(t)).start())
+        for part, (low, high) in enumerate(ranges):
+            pass_range(1, part, low, high)
             weight_part(glp, (2,), low, high, low == 0)
         store_shares(1, 1, 0)
         begin(scatter(1, 1))
+        forward_grad(1, 0, every).wait_recv()
         loop(0, turns, lambda t: product(1, t, False))
         end_hop(0)
-        sum_shares(1, 1)
-
-        def last_turn(t):
-            pass_on(2, t)
-
-            @pl.when(t >= 2)
-            def _():
-                product(2, t - 2, False)
-
-        for low, high in ranges:
-            loop(low, high, last_turn)
-            weight_part(glp, (3,), low, high, low == 0)
-        store_shares(2, 1, 0)
-        begin(scatter(2, 1))
-        for t in (turns - 2, turns - 1):
-            product(2, t, False)
-        end_hop(1)
 
         def link_copy(g):
             return pltpu.make_async_copy(
@@ -1567,7 +1586,30 @@
             link_total[...] += dot(link, gbuf[g % 2])
             slot_copy(g).start()
 
-        loop(0, groups, slot_group)
+        def slots_done(t):
+            return (3 * t) // 4
+
+        def last_turn(t):
+            @pl.when(t >= 1)
+            def _():
+                forward_grad(2, t - 1, at(t - 1)).wait_recv()
+                product(2, t - 1, False)
+                loop(slots_done(t - 1), slots_done(t), slot_group)
+
+            send_grad(2, t, at(t)).wait_recv()
+            forward_grad(2, t, at(t)).start()
+
+        for low, high in ranges:
+            loop(low, high, last_turn)
+            weight_part(glp, (3,), low, high, low == 0)
+            if low == 5:
+                sum_shares(1, 1)
+        store_shares(2, 1, 0)
+        begin(scatter(2, 1))
+        end_hop(1)
+        forward_grad(2, turns - 1, at(turns - 1)).wait_recv()
+        product(2, turns - 1, False)
+        loop(slots_done(turns - 1), groups, slot_group)
         hbuf[...] = link_total[...].astype(bf16)
         half = hbuf.shape[0] // 2
         returns = [
@@ -1581,17 +1623,13 @@
         finish(returns)
         back_ref[:half, :] = jnp.where(me == nodes - 1, 0.0, hback[:half, :].astype(f32)).astype(bf16)
         back_ref[half:, :] = jnp.where(me == 0, 0.0, hback[half:, :].astype(f32)).astype(bf16)
-        end_hop(2)
-
-        def settle(t):
-            send_own(t).wait_send()
-            for b in range(2):
-                give_grad(b, t).wait_send()
-            for p in range(3):
-                send_grad(p, t).wait_send()
-                forward_grad(p, t).wait_send()
-
-        loop(0, turns, settle)
+
+        send_own(0, every).wait_send()
+        for b in range(2):
+            give_grad(b, every).wait_send()
+        for p in range(3):
+            send_grad(p, 0, every).wait_send()
+            forward_grad(p, 0, every).wait_send()
         for p in range(3):
             for kind in range(2):
                 finish_spread(p, kind)
@@ -1620,10 +1658,10 @@
         pltpu.VMEM((4, nodes, LANE, LANE), bf16),
         pltpu.VMEM((2, nodes, wide, LANE), bf16),
         pltpu.VMEM((4, nodes, LANE, LANE), bf16),
-        pltpu.VMEM((1, LANE, wide), bf16),
-        pltpu.VMEM((2, LANE, LANE), bf16),
         pltpu.VMEM((2, LANE, wide), bf16),
         pltpu.VMEM((4, LANE, LANE), bf16),
+        pltpu.VMEM((LANE, wide), bf16),
+        pltpu.VMEM((LANE, LANE), bf16),
         pltpu.VMEM((3, team * SLOT, fw), bf16),
         pltpu.VMEM((3, team, 3 * SLOT, SLOT), bf16),
         pltpu.VMEM((2, team * SLOT, wide), bf16),
@@ -1642,24 +1680,22 @@
         dma((2,)),
         dma((2,)),
         dma((2,)),
+        dma((1,)),
         dma((turns,)),
-        dma((turns,)),
-        dma((2 * turns,)),
-        dma((2 * turns,)),
-        dma((3 * turns,)),
-        dma((3 * turns,)),
-        dma((2 * turns,)),
-        dma((2 * turns,)),
-        dma((3 * turns,)),
-        dma((3 * turns,)),
-        dma((4 * nodes,)),
-        dma((4 * nodes,)),
-        dma((6 * nodes,)),
-        dma((6 * nodes,)),
+        dma((2,)),
+        dma((6,)),
         dma((3,)),
+        dma((6 + turns,)),
+        dma((2,)),
+        dma((2,)),
         dma((3,)),
-        dma((6 * nodes,)),
-        dma((6 * nodes,)),
+        dma((2 + turns,)),
+        dma((4,)),
+        dma((4,)),
+        dma((6,)),
+        dma((6,)),
+        dma((6,)),
+        dma((6,)),
         dma((4,)),
         dma((4,)),
         dma((6,)),
@@ -1670,10 +1706,14 @@
         pltpu.VMEM((2 * fw, fw), bf16),
         pltpu.VMEM((2 * fw, fw), bf16),
         dma((2 * quarter,)),
-        dma((4,)),
-        dma((4,)),
+        dma((3,)),
+        dma((3,)),
         pltpu.VMEM((2 * SLOT, fw), bf16),
         pltpu.VMEM((slots, 8, SLOT), f32),
+        dma((2,)),
+        dma((2,)),
+        dma((2,)),
+        dma((2,)),
     ]
     return pl.pallas_call(
         kernel,

time: 317 us -> 301 us (0.950)
  Pallas kernels: 311 us -> 295 us
    pallas_call x1, Pallas kernels: 290 us -> 274 us  [core(): pl.pallas_call(kernel, out_shape=outs, in_specs=[smem()] * 3 + [anywhere]...]
where the time goes in v1:
time: 301 us; the launch traced here: 300 us
  Pallas kernels  295 us (98%)
    pallas_call x1, Pallas kernels, core(): pl.pallas_call(kernel, out_shape=outs, in_specs=[smem()] * 3 + [anywhere]...  274 us
    pallas_call x1, Pallas kernels, last_pass(): pl.pallas_call(kernel, grid=(nodes,), out_shape=[jax.ShapeDtypeStruct((ro...  20.9 us

profile of v1, /device:TPU:0, one launch (start us, length us, event | category | flops | bytes accessed | tf_op | source)
XLA Modules:
  0.0 300.4 jit_solution(5063384030345064148)
XLA Ops:
  0.6 0.8 bitcast_reduce_fusion.refs_1_
  1.5 0.1 select_reduce_fusion.refs_0_
  1.6 0.1 slice.70
  1.7 0.2 convert_reduce_fusion
  1.8 0.5 broadcast_minimum_fusion.refs_2_
  2.4 0.8 slice_bitcast_fusion.3
  3.1 0.0 copy-start.17
  3.1 0.0 copy-start.21
  3.2 0.0 copy-start.23
  3.2 0.0 copy-start.24
  3.2 0.0 copy-start.25
  3.2 274.3 %core.1 = (f32[6144,512]{1,0:T(8,128)}, bf16[6144,512]{1,0:T(8,128)(2,1)}, bf16[256,512]{1,0:T(8,128)(2,1)}, bf16[8,2,128,512]{3,2,1,0:T(8,128)(2,1)}, f32[8,512...) custom-call(s32[49]{0:T(128)S(1)} %select_reduce_fusion.refs_0_, s32[48]{0:T(128)S(1)} %bitcast_reduce_fusion.refs_1_, ...), custom_call_target="tpu_custom_call" | custom-call | flops 1 | bytes 1 | tf_op jit(solution)/shard_map/core/pallas_call | solution.py:1718
  277.5 0.5 slice.73
  278.6 0.0 copy-done.17
  278.6 0.0 copy-done.21
  278.7 0.0 copy-done.23
  278.7 0.0 copy-done.24
  278.7 0.0 copy-done.25
  278.7 21.8 %conditional.1 = (f32[6144,512]{1,0:T(8,128)}, f32[6144,512]{1,0:T(8,128)}, f32[2048,512]{1,0:T(8,128)}, f32[512]{0:T(512)}, f32[512]{0:T(512)}) conditional(s32[]{:T(128)} %bitcast.29, (s32[48]{0:T(128)S(1)}, s32[16,6144]{1,0:T(8,128)S(1)}, s32[4,6144]{1,0:T(4,128)S(1)}, s32[256]{0:T(256)S(1)}, bf16[6144,512]{1,0:T(8,128)(2,1)}, ...), branch_computations={%region_3.4_spmd, %region_4.5_spmd} | conditional | flops 12897878016 | bytes 500249184 | solution.py:1848
  279.0 20.9 %last_pass.1 = (f32[6144,512]{1,0:T(8,128)}, f32[6144,512]{1,0:T(8,128)}, f32[2,8,128,512]{3,2,1,0:T(8,128)}) custom-call(s32[48]{0:T(128)S(1)} %get-tuple-element.67.counts_ref, f32[6144,512]{1,0:T(8,128)} %get-tuple-element.68.act_ref, bf16[6144,512]{1,0:T(8,128)(2,1)} %get-tuple-element.69.grad_ref, bf16[48,384,128]{2,1,0:T(8,128)(2,1)} %get-tuple-element.70.tile_ref, ...), custom_call_target="tpu_custom_call" | custom-call | flops 1 | bytes 1 | tf_op jit(solution)/shard_map/cond/branch_1_fun/last_pass/pallas_call | solution.py:746
  299.9 0.6 fusion.12
  (3 shorter events, 0.0 us)
Async XLA Ops:
  3.1 275.5 %copy-start.17 = (s32[6144,16]{0,1:T(8,128)S(1)}, s32[6144,16]{0,1:T(8,128)}, u32[]{:S(2)}) copy-start(s32[6144,16]{0,1:T(8,128)} %param.16) | copy-start | bytes 1179652
  3.1 275.5 %copy-start.21 = (s32[6144,4]{0,1:T(4,128)S(1)}, s32[6144,4]{0,1:T(4,128)}, u32[]{:S(2)}) copy-start(s32[6144,4]{0,1:T(4,128)} %param.17) | copy-start | bytes 294916
  3.2 275.5 %copy-start.23 = (s32[6144]{0:T(1024)S(1)}, s32[6144]{0:T(1024)}, u32[]{:S(2)}) copy-start(s32[6144]{0:T(1024)} %param.18) | copy-start | bytes 73732
  3.2 275.5 %copy-start.24 = (f32[512]{0:T(512)S(1)}, f32[512]{0:T(512)}, u32[]{:S(2)}) copy-start(f32[512]{0:T(512)} %param.13) | copy-start | bytes 6148
  3.2 275.5 %copy-start.25 = (f32[512]{0:T(512)S(1)}, f32[512]{0:T(512)}, u32[]{:S(2)}) copy-start(f32[512]{0:T(512)} %param.14) | copy-start | bytes 6148

commit v2 on v1

--- a/solution.py
+++ b/solution.py
@@ -719,15 +719,16 @@
     )(counts, slot_grad, tiles, returned, send_row)
 
 
-def last_pass(act, slot_grad, returned, shares, tiles, send_row, counts):
+def last_pass(act, slot_grad, returned, shares, tiles, send_pairs, counts):
     rows, width = slot_grad.shape
-    sends = send_row.shape[1]
+    sends = 2 * send_pairs.shape[1]
     nodes = shares.shape[0]
     group = rows // SLOT // nodes
 
     def kernel(counts_ref, act_ref, grad_ref, tile_ref, back_ref, send_ref, share_ref, *outs):
         act_out, grad_out, weight_out = outs
         step = pl.program_id(0)
+        wanted = jnp.concatenate([send_ref[1:2, :], send_ref[0:1, :]], 1)
         act_out[...] = act_ref[...]
         weight_out[...] = share_ref[...].astype(f32).reshape(weight_out.shape)
 
@@ -736,7 +737,7 @@
                 member = turn * 2 + side
                 slot = step * group + member
                 here = pl.ds(pl.multiple_of(member * SLOT, SLOT), SLOT)
-                hot = chosen(send_ref, slot * SLOT, SLOT, counts_ref[slot])
+                hot = chosen(wanted, slot * SLOT, SLOT, counts_ref[slot])
                 value = dot(tile_ref[member], grad_ref[here, :])
                 grad_out[here, :] = value + dot(hot, back_ref[...])
             return carry
@@ -757,7 +758,7 @@
             pl.BlockSpec((group * SLOT, width), lambda i: (i, 0)),
             pl.BlockSpec((group, SLOT, SLOT), lambda i: (i, 0, 0)),
             fixed((sends, width)),
-            fixed((1, sends)),
+            fixed(send_pairs.shape),
             pl.BlockSpec((1, 2, LANE, width), lambda i: (i, 0, 0, 0)),
         ],
         out_specs=[
@@ -768,7 +769,7 @@
         compiler_params=params(),
         cost_estimate=cost(0, 0),
         name="last_pass",
-    )(counts, act, slot_grad, tiles, returned, send_row, shares)
+    )(counts, act, slot_grad, tiles, returned, send_pairs, shares)
 
 
 def node_shift(block, distance):
@@ -816,7 +817,7 @@
 
 
 def core(
-    features, weight, cotangent, near, links, send_row, scale, shift, lists, nodes, compact
+    features, weight, cotangent, near, links, send_pairs, scale, shift, lists, nodes, compact
 ):
     rows, fw = features.shape
     entries, link_entries = near.shape[0], links.shape[0]
@@ -1021,7 +1022,7 @@
         wanted = [
             jnp.transpose(
                 jnp.broadcast_to(
-                    send_ref[:, part * LANE : (part + 1) * LANE].astype(f32), (LANE, LANE)
+                    send_ref[1 - part : 2 - part, :].astype(f32), (LANE, LANE)
                 )
             )
             for part in range(2)
@@ -1140,30 +1141,39 @@
                     own[into, q * LANE : (q + 1) * LANE] = pick(q).astype(bf16)
             send_own(t).start()
 
-            @pl.when(t == 1)
+            @pl.when(t > done_before[0])
+            def _():
+                first_partial(t - 1)
+
+        done_before = [0]
+
+        def ready(g):
+            return jnp.where(g == groups - 1, turns, jnp.minimum((team * (g + 1)) // 6, turns))
+
+        def gather_group(g):
+            @pl.when(g + 2 < groups)
+            def _():
+                loads(g + 2).start()
+
+                @pl.when(g >= 1)
+                def _():
+                    tile_copy(g - 1).wait()
+
+                count_group(g + 2)
+
+            done = jnp.where(g == 0, 0, jnp.minimum((team * g) // 6, turns))
+            earlier = jnp.where(g <= 1, 0, jnp.minimum((team * (g - 1)) // 6, turns))
+
+            @pl.when(g == 2)
             def _():
                 send_weight_share(1).wait_recv()
                 spread_weights(1)
                 send_upper_weights().wait_recv()
                 spread_weights_end(0).wait_recv()
 
-            @pl.when(t >= 1)
+            @pl.when(done > earlier)
             def _():
-                first_partial(t - 1)
-
-        def ready(g):
-            return jnp.where(g == groups - 1, turns, jnp.minimum((team * (g + 1)) // 6, turns))
-
-        def gather_group(g):
-            @pl.when(g + 2 < groups)
-            def _():
-                loads(g + 2).start()
-
-                @pl.when(g >= 1)
-                def _():
-                    tile_copy(g - 1).wait()
-
-                count_group(g + 2)
+                first_partial(done - 1)
 
             loads(g).wait()
             spot = g % 3
@@ -1176,7 +1186,7 @@
                 into = pl.ds(pl.multiple_of((slot + 1) * SLOT, SLOT), SLOT)
                 for q in range(quarter):
                     big[q, into, :] = value[:, q * LANE : (q + 1) * LANE] * scale
-            done = jnp.where(g == 0, 0, jnp.minimum((team * g) // 6, turns))
+            done_before[0] = done
             loop(done, ready(g), compact_tile)
 
         loop(0, groups, gather_group)
@@ -1726,18 +1736,20 @@
         ),
         cost_estimate=cost(0, 0),
         name="core",
-    )(*lists, features, weight, cotangent, near, links, send_row, gain, bias)
+    )(*lists, features, weight, cotangent, near, links, send_pairs, gain, bias)
 
 
 def every_row(
-    features, weight, cotangent, near, links, send_list, valid_row, scale, shift, lists, nodes, chips
+    features, weight, cotangent, near, links, send_pairs, valid_rows, scale, shift, lists, nodes, chips
 ):
     offsets, counts = lists[:2]
     rows, fw = features.shape
     slots = rows // SLOT
     chip, core_side = lax.axis_index("mp") // 2, lax.rem(lax.axis_index("mp"), 2)
     core_word = core_side.astype(i32)[None]
-    half = send_list.shape[0] // 2
+    half = send_pairs.shape[1]
+    send_list = jnp.concatenate([send_pairs[1], send_pairs[0]], 0)
+    valid_row = valid_rows[None, :].astype(i32)
     others = range(1, chips)
     wide = fw // 2
 
@@ -1827,22 +1839,20 @@
     ).astype(i32)
     lists = (offsets, counts, first)
     near, links = neighbours.T, halo_links.T
-    send_list = jnp.concatenate([send_rows[:, 1], send_rows[:, 0]], 0)
-    valid_row = valid_rows[None, :].astype(i32)
+    send_pairs = send_rows.T
 
     def all_rows(*args):
         return every_row(*args, lists, nodes, chips)
 
-    given = (features, weight, cotangent, near, links, send_list, valid_row, scale, shift)
+    given = (features, weight, cotangent, near, links, send_pairs, valid_rows, scale, shift)
     if not (chips == 2 and fw == 4 * LANE and 2 * fw == nodes * LANE and slots % nodes == 0):
         return all_rows(*given)
-    send_row = send_list[None, :]
     *made, totals, tiles = core(
-        features, weight, cotangent, near, links, send_row, scale, shift, lists, nodes, compact
+        features, weight, cotangent, near, links, send_pairs, scale, shift, lists, nodes, compact
     )
 
     def few_rows(*args):
-        act, input_grad, weight_grad = last_pass(*made, tiles, send_row, counts)
+        act, input_grad, weight_grad = last_pass(*made, tiles, send_pairs, counts)
         return act, input_grad, weight_grad.reshape(mp * fw, fw), totals[0], totals[1]
 
     return lax.cond(totals[2, 0] <= compact, few_rows, all_rows, *given)

time: 301 us -> 299 us (level)
  no operation moved by 1% of the time
where the time goes in v2:
time: 299 us; the launch traced here: 298 us
  Pallas kernels  294 us (98%)
    pallas_call x1, Pallas kernels, core(): pl.pallas_call(kernel, out_shape=outs, in_specs=[smem()] * 3 + [anywhere]...  273 us
    pallas_call x1, Pallas kernels, last_pass(): pl.pallas_call(kernel, grid=(nodes,), out_shape=[jax.ShapeDtypeStruct((ro...  20.9 us

profile of v2, /device:TPU:0, one launch (start us, length us, event | category | flops | bytes accessed | tf_op | source)
XLA Modules:
  0.0 298.3 jit_solution(17607185425920767161)
XLA Ops:
  0.6 0.8 bitcast_reduce_fusion.refs_1_
  1.5 0.1 select_reduce_fusion.refs_0_
  1.6 0.1 slice.70
  1.7 0.2 convert_reduce_fusion
  1.8 0.5 broadcast_minimum_fusion.refs_2_
  2.4 0.0 copy-start.17
  2.4 0.0 copy-start.21
  2.4 0.0 copy-start.23
  2.4 0.0 copy-start.24
  2.4 0.0 copy-start.25
  2.4 0.0 copy-start.26
  2.4 272.9 %core.1 = (f32[6144,512]{1,0:T(8,128)}, bf16[6144,512]{1,0:T(8,128)(2,1)}, bf16[256,512]{1,0:T(8,128)(2,1)}, bf16[8,2,128,512]{3,2,1,0:T(8,128)(2,1)}, f32[8,512...) custom-call(s32[49]{0:T(128)S(1)} %select_reduce_fusion.refs_0_, s32[48]{0:T(128)S(1)} %bitcast_reduce_fusion.refs_1_, ...), custom_call_target="tpu_custom_call" | custom-call | flops 1 | bytes 1 | tf_op jit(solution)/shard_map/core/pallas_call | solution.py:1728
  275.3 0.5 slice.71
  276.4 0.0 copy-done.17
  276.4 0.0 copy-done.21
  276.5 0.0 copy-done.23
  276.5 0.0 copy-done.24
  276.5 0.0 copy-done.25
  276.5 0.0 copy-done.26
  276.5 21.8 %conditional.1 = (f32[6144,512]{1,0:T(8,128)}, f32[6144,512]{1,0:T(8,128)}, f32[2048,512]{1,0:T(8,128)}, f32[512]{0:T(512)}, f32[512]{0:T(512)}) conditional(s32[]{:T(128)} %bitcast.29, (s32[48]{0:T(128)S(1)}, s32[16,6144]{1,0:T(8,128)S(1)}, s32[4,6144]{1,0:T(4,128)S(1)}, s32[2,128]{1,0:T(2,128)S(1)}, s32[6144]{0:T(1024)S(1)}, ...), branch_computations={%region_3.4_spmd, %region_4.5_spmd} | conditional | flops 12897878016 | bytes 500257408 | solution.py:1858
  276.8 20.9 %last_pass.1 = (f32[6144,512]{1,0:T(8,128)}, f32[6144,512]{1,0:T(8,128)}, f32[2,8,128,512]{3,2,1,0:T(8,128)}) custom-call(s32[48]{0:T(128)S(1)} %get-tuple-element.67.counts_ref, f32[6144,512]{1,0:T(8,128)} %get-tuple-element.68.act_ref, bf16[6144,512]{1,0:T(8,128)(2,1)} %get-tuple-element.69.grad_ref, bf16[48,384,128]{2,1,0:T(8,128)(2,1)} %get-tuple-element.70.tile_ref, ...), custom_call_target="tpu_custom_call" | custom-call | flops 1 | bytes 1 | tf_op jit(solution)/shard_map/cond/branch_1_fun/last_pass/pallas_call | solution.py:747
  297.7 0.6 fusion.12
  (2 shorter events, 0.0 us)
Async XLA Ops:
  2.4 274.1 %copy-start.17 = (s32[6144,16]{0,1:T(8,128)S(1)}, s32[6144,16]{0,1:T(8,128)}, u32[]{:S(2)}) copy-start(s32[6144,16]{0,1:T(8,128)} %param.16) | copy-start | bytes 1179652
  2.4 274.1 %copy-start.21 = (s32[6144,4]{0,1:T(4,128)S(1)}, s32[6144,4]{0,1:T(4,128)}, u32[]{:S(2)}) copy-start(s32[6144,4]{0,1:T(4,128)} %param.17) | copy-start | bytes 294916
  2.4 274.1 %copy-start.23 = (s32[6144]{0:T(1024)S(1)}, s32[6144]{0:T(1024)}, u32[]{:S(2)}) copy-start(s32[6144]{0:T(1024)} %param.18) | copy-start | bytes 73732
  2.4 274.1 %copy-start.24 = (f32[512]{0:T(512)S(1)}, f32[512]{0:T(512)}, u32[]{:S(2)}) copy-start(f32[512]{0:T(512)} %param.13) | copy-start | bytes 6148
  2.4 274.1 %copy-start.25 = (f32[512]{0:T(512)S(1)}, f32[512]{0:T(512)}, u32[]{:S(2)}) copy-start(f32[512]{0:T(512)} %param.14) | copy-start | bytes 6148
  2.4 274.1 %copy-start.26 = (s32[128,2]{0,1:T(2,128)S(1)}, s32[128,2]{0,1:T(2,128)}, u32[]{:S(2)}) copy-start(s32[128,2]{0,1:T(2,128)} %param.19) | copy-start | bytes 3076
